TPU v7x, 32 devices: a whole 2x2x4 slice. The times are simulated.
32 devices in a mesh: grp: 4 (over x, core), dev: 8 (over z, y).
Axes of the slice: x: 2, y: 2, z: 4, core: 2. Of those that a mesh axis runs over, the one named last changes fastest.
Arguments:
- home_points: bfloat16 [65536, 512], P(('grp', 'dev')), may hold values from -6 to 6
- counts: int32 [32], P(('grp', 'dev')), may hold values from 0 to 2, as said below
- owner_group: int32 [64], P(('grp', 'dev')), may hold values from 0 to 3, as said below
- neighbors_home: int32 [27, 65536], P(None, ('grp', 'dev')), may hold values from 0 to 1023
- hilbert_target: int32 [512], P(('grp', 'dev')), may hold values from 0 to 127, as said below
- neighbors_second: int32 [27, 32768], P(None, ('grp', 'dev')), may hold values from 0 to 1023
- depth_first: float32 [27, 512], replicated, may hold values from -1.5 to 1.5
- mixing_first: bfloat16 [512, 512], replicated, may hold values from -0.25 to 0.25
- gain_first: float32 [512], replicated, may hold values from 0.1 to 1.9
- w_qkv_first: bfloat16 [512, 1536], replicated, may hold values from -3 to 3
- w_out_first: bfloat16 [512, 512], replicated, may hold values from -0.25 to 0.25
- depth_second: float32 [27, 512], replicated, may hold values from -1.5 to 1.5
- mixing_second: bfloat16 [512, 512], replicated, may hold values from -0.25 to 0.25
- gain_second: float32 [512], replicated, may hold values from 0.1 to 1.9
- w_qkv_second: bfloat16 [512, 1536], replicated, may hold values from -3 to 3
- w_out_second: bfloat16 [512, 512], replicated, may hold values from -0.25 to 0.25
Outputs:
- encoded_points: bfloat16 [65536, 512], P(('grp', 'dev'))
Inputs may be any that keep to these rules, and one draw needn't show every extreme that they name: For each dev index, the counts of its 4 tiles sum to 4. `owner_group`: the live slots of one tile name distinct groups, and for each dev index d and group q exactly one live slot of the tiles with dev index d names q. Dead slots' values are unused. `hilbert_target`: within each group the targets are a permutation of 0 to 127, and at most 2 blocks of one device name the same device (target // 16).
All inputs are finite; a program needn't handle non-finite values.
Results may differ from a plain program's by a relative error of at most 0.025.
Values may be sent and summed in bfloat16 or wider, within the bound.
A program may use at most 128 MiB of HBM per device.

v0:
```python
import functools
import math

import jax
import jax.numpy as jnp
from jax import lax
from jax.experimental import pallas as pl
from jax.experimental.pallas import tpu as pltpu
from jax.sharding import PartitionSpec as P

HEADS = 8
HEAD_DIM = 64
CAPACITY = 2
CORES = 2
CHUNK = 256
EPSILON = 1e-05
ONES = 16


def block_kernel(
    fetch_ref,
    order_ref,
    source_ref,
    lists_ref,
    depth_ref,
    mixing_ref,
    gain_ref,
    qkv_ref,
    out_w_ref,
    out_ref,
    x_ref,
    xt_ref,
    wide_ref,
    acc_ref,
    code_ref,
    updated_ref,
    qt_ref,
    k_ref,
    vt_ref,
    mixed_ref,
    result_ref,
):
    rows, width = x_ref.shape
    fanout = depth_ref.shape[1]
    in_blocks = fetch_ref.shape[0]
    out_blocks = order_ref.shape[0]
    piece = rows // in_blocks
    chunks = rows // CHUNK
    for b in range(in_blocks):
        x_ref[pl.ds(b * piece, piece), :] = source_ref[
            pl.ds(pl.multiple_of(fetch_ref[b] * piece, piece), piece), :
        ]
    xt_ref[...] = x_ref[...].T
    for j in range(fanout):
        wide_ref[j] = jnp.broadcast_to(depth_ref[:, j : j + 1], (width, 128))
    places = lax.broadcasted_iota(jnp.int32, (rows, CHUNK), 0).astype(jnp.int16)

    @pl.loop(0, chunks)
    def _(c):
        at = pl.multiple_of(c * CHUNK, CHUNK)
        acc_ref[...] = jnp.zeros_like(acc_ref)

        @pl.loop(0, fanout, step=3)
        def _(j0):
            total = acc_ref[...]
            for dj in range(3):
                j = j0 + dj
                row = lists_ref[pl.ds(j, 1), pl.ds(at, CHUNK)].astype(jnp.int16)
                hot = jnp.where(places == row, 1.0, 0.0).astype(jnp.bfloat16)
                got = jnp.dot(xt_ref[...], hot, preferred_element_type=jnp.float32)
                weight = wide_ref[j]
                total = total + got * jnp.concatenate([weight] * (CHUNK // 128), axis=1)
            acc_ref[...] = total

        code_ref[pl.ds(at, CHUNK), :] = acc_ref[...].T.astype(jnp.bfloat16)

    gain = gain_ref[...]
    scale = HEAD_DIM**-0.5 * math.log2(math.e)

    @pl.loop(0, chunks)
    def _(c):
        here = pl.ds(pl.multiple_of(c * CHUNK, CHUNK), CHUNK)
        updated = x_ref[here, :].astype(jnp.float32) + jnp.dot(
            code_ref[here, :], mixing_ref[...], preferred_element_type=jnp.float32
        )
        updated_ref[here, :] = updated
        centre = jnp.mean(updated, axis=-1, keepdims=True)
        moved = updated - centre
        spread = jnp.mean(moved * moved, axis=-1, keepdims=True)
        normed = (moved * lax.rsqrt(spread + EPSILON) * gain).astype(jnp.bfloat16)
        project = jnp.dot(normed, qkv_ref[...], preferred_element_type=jnp.float32)
        qt_ref[:, here] = (project[:, :width] * scale).T.astype(jnp.bfloat16)
        k_ref[here, :] = project[:, width : 2 * width].astype(jnp.bfloat16)
        values = project[:, 2 * width :].T.astype(jnp.bfloat16)
        for h in range(HEADS):
            vt_ref[h, :HEAD_DIM, here] = values[h * HEAD_DIM : (h + 1) * HEAD_DIM]

    vt_ref[:, HEAD_DIM:, :] = jnp.ones((HEADS, ONES, rows), jnp.bfloat16)

    @pl.loop(0, chunks)
    def _(c):
        here = pl.ds(pl.multiple_of(c * CHUNK, CHUNK), CHUNK)
        for h in range(HEADS):
            pair = h // 2
            zero = jnp.zeros((HEAD_DIM, CHUNK), jnp.bfloat16)
            query = qt_ref[pl.ds(h * HEAD_DIM, HEAD_DIM), here]
            padded = jnp.concatenate([query, zero] if h % 2 == 0 else [zero, query], axis=0)
            scores = jnp.dot(
                k_ref[:, pair * 128 : (pair + 1) * 128], padded, preferred_element_type=jnp.float32
            )
            peak = jnp.max(scores, axis=0, keepdims=True)
            powers = jnp.exp2(scores - peak).astype(jnp.bfloat16)
            mixed = jnp.dot(vt_ref[h], powers, preferred_element_type=jnp.float32)
            mixed_ref[pl.ds(h * HEAD_DIM, HEAD_DIM), :] = (
                mixed[:HEAD_DIM] / mixed[HEAD_DIM : HEAD_DIM + 1]
            )
        mixed = mixed_ref[...].T.astype(jnp.bfloat16)
        result_ref[here, :] = (
            updated_ref[here, :]
            + jnp.dot(mixed, out_w_ref[...], preferred_element_type=jnp.float32)
        ).astype(jnp.bfloat16)

    for b in range(out_blocks):
        out_ref[pl.ds(b * piece, piece), :] = result_ref[
            pl.ds(pl.multiple_of(order_ref[b] * piece, piece), piece), :
        ]


def run_block(source, lists, params, fetch, order, rows):
    depth, mixing, gain, w_qkv, w_out = params
    width = source.shape[1]
    fanout = lists.shape[0]
    piece = rows // fetch.shape[0]
    vmem = pl.BlockSpec(memory_space=pltpu.VMEM)
    smem = pl.BlockSpec(memory_space=pltpu.SMEM)
    return pl.pallas_call(
        block_kernel,
        out_shape=jax.ShapeDtypeStruct((order.shape[0] * piece, width), jnp.bfloat16),
        in_specs=[smem, smem] + [vmem] * 7,
        out_specs=vmem,
        scratch_shapes=[
            pltpu.VMEM((rows, width), jnp.bfloat16),
            pltpu.VMEM((width, rows), jnp.bfloat16),
            pltpu.VMEM((fanout, width, 128), jnp.float32),
            pltpu.VMEM((width, CHUNK), jnp.float32),
            pltpu.VMEM((rows, width), jnp.bfloat16),
            pltpu.VMEM((rows, width), jnp.float32),
            pltpu.VMEM((width, rows), jnp.bfloat16),
            pltpu.VMEM((rows, width), jnp.bfloat16),
            pltpu.VMEM((HEADS, HEAD_DIM + ONES, rows), jnp.bfloat16),
            pltpu.VMEM((width, CHUNK), jnp.float32),
            pltpu.VMEM((rows, width), jnp.bfloat16),
        ],
        compiler_params=pltpu.CompilerParams(vmem_limit_bytes=56 * 1024 * 1024),
        cost_estimate=pl.CostEstimate(
            flops=2 * fanout * rows * rows * width, bytes_accessed=8 << 20, transcendentals=8 << 20
        ),
        name="block",
    )(fetch, order, source, lists, depth.T, mixing, gain.reshape(1, width), w_qkv, w_out)


def body(
    home_points,
    counts,
    owner_group,
    neighbors_home,
    hilbert_target,
    neighbors_second,
    depth_first,
    mixing_first,
    gain_first,
    w_qkv_first,
    w_out_first,
    depth_second,
    mixing_second,
    gain_second,
    w_qkv_second,
    w_out_second,
):
    groups = lax.axis_size("grp")
    owners = lax.axis_size("dev")
    chips = groups // CORES
    me = lax.axis_index("grp")
    place_x, core = me // CORES, me % CORES
    mine = lax.axis_index("dev")
    home_rows, width = home_points.shape
    slot_count = owner_group.shape[0]
    rows = home_rows // slot_count
    block_count = hilbert_target.shape[0]
    piece = rows // block_count
    fanout = neighbors_home.shape[0]
    mate = [(i, i ^ 1) for i in range(groups)]
    first_params = (depth_first, mixing_first, gain_first, w_qkv_first, w_out_first)
    second_params = (depth_second, mixing_second, gain_second, w_qkv_second, w_out_second)

    targets = lax.all_gather(hilbert_target, "dev", axis=0, tiled=True).reshape(
        owners, block_count
    )

    filled = jnp.arange(slot_count) < counts[0]
    wanted = jnp.where(filled, owner_group, -1)
    tiles = home_points.reshape(slot_count, rows, width)
    lists = jnp.transpose(neighbors_home.reshape(fanout, slot_count, rows), (1, 0, 2))
    stamped = jnp.concatenate(
        [lists, jnp.broadcast_to(wanted[:, None, None], (slot_count, 1, rows))], axis=1
    )
    other_tiles = lax.ppermute(tiles, "grp", mate)
    other_stamped = lax.ppermute(stamped, "grp", mate)
    other_wanted = other_stamped[:, fanout, 0]

    def candidate(target):
        here, there = wanted == target, other_wanted == target
        at_here = jnp.sum(jnp.where(here, jnp.arange(slot_count), 0))
        at_there = jnp.sum(jnp.where(there, jnp.arange(slot_count), 0))
        ours = jnp.any(here)
        pick = lambda a, b: jnp.where(
            ours,
            lax.dynamic_index_in_dim(a, at_here, 0, keepdims=False),
            lax.dynamic_index_in_dim(b, at_there, 0, keepdims=False),
        )
        return ours | jnp.any(there), pick(tiles, other_tiles), pick(stamped, other_stamped)

    held, points, stamps = candidate(me)
    for r in range(1, chips):
        target = ((place_x + r) % chips) * CORES + core
        _, points_out, stamps_out = candidate(target)
        over = [
            (x * CORES + c, ((x + r) % chips) * CORES + c)
            for x in range(chips)
            for c in range(CORES)
        ]
        points_in = lax.ppermute(points_out, "grp", over)
        stamps_in = lax.ppermute(stamps_out, "grp", over)
        take = stamps_in[fanout, 0] == me
        points = jnp.where(take, points_in, points)
        stamps = jnp.where(take, stamps_in, stamps)

    slots = owners * CAPACITY
    counter = jnp.arange(block_count)
    destination = targets // block_count
    same = destination[:, :, None] == destination[:, None, :]
    rank = jnp.sum(same & (counter[:, None] > counter[None, :]), axis=2)
    places = destination * CAPACITY + rank
    place = lax.dynamic_index_in_dim(places, mine, 0, keepdims=False)
    order = jnp.sum(
        jnp.where(place[None, :] == jnp.arange(slots)[:, None], counter[None, :], 0), axis=1
    ).astype(jnp.int32)
    sent_at = (jnp.arange(owners)[:, None] * CAPACITY + rank).reshape(-1)
    flat = targets.reshape(-1)
    goal = mine * block_count + counter
    fetch = jnp.sum(
        jnp.where(flat[None, :] == goal[:, None], sent_at[None, :], 0), axis=1
    ).astype(jnp.int32)
    back = jnp.sum(
        jnp.where(fetch[None, :] == jnp.arange(slots)[:, None], counter[None, :], 0), axis=1
    ).astype(jnp.int32)

    straight = jnp.arange(block_count, dtype=jnp.int32)
    outgoing = run_block(points, stamps[:fanout], first_params, straight, order, rows)
    swap = lambda a: lax.all_to_all(a, "dev", split_axis=0, concat_axis=0, tiled=True)
    incoming = swap(outgoing)
    backward = run_block(incoming, neighbors_second, second_params, fetch, back, rows)
    returned = swap(backward).reshape(slots, piece, width)
    finished = returned[place].reshape(rows, width)

    gathered = [finished]
    for r in range(1, chips):
        over = [
            (x * CORES + c, ((x + r) % chips) * CORES + c)
            for x in range(chips)
            for c in range(CORES)
        ]
        gathered.append(lax.ppermute(finished, "grp", over))
    stack = jnp.stack(gathered)
    other = lax.ppermute(stack, "grp", mate)
    shift = (place_x - owner_group // CORES) % chips
    ours = owner_group % CORES == core
    parts = [
        jnp.where(
            filled[s],
            jnp.where(
                ours[s],
                lax.dynamic_index_in_dim(stack, shift[s], 0, keepdims=False),
                lax.dynamic_index_in_dim(other, shift[s], 0, keepdims=False),
            ),
            jnp.zeros((), jnp.bfloat16),
        )
        for s in range(slot_count)
    ]
    return jnp.concatenate(parts, axis=0)


def solution(mesh):
    return jax.shard_map(
        body,
        mesh=mesh,
        in_specs=(
            P(("grp", "dev"), None),
            P(("grp", "dev")),
            P(("grp", "dev")),
            P(None, ("grp", "dev")),
            P(("grp", "dev")),
            P(None, ("grp", "dev")),
            P(),
            P(),
            P(),
            P(),
            P(),
            P(),
            P(),
            P(),
            P(),
            P(),
        ),
        out_specs=P(("grp", "dev"), None),
        check_vma=False,
    )
```

profile of v0, /device:TPU:25, one launch (start us, length us, event | category | flops | bytes accessed | tf_op | source)
XLA Modules:
  0.0 298.6 jit_solution(4573247589447827808)
XLA Ops:
  0.0 0.7 collective-permute-start.2
  1.3 1.1 reshape.171
  2.5 0.1 copy.26
  2.6 1.3 compare_reduce_fusion.2
  3.9 0.1 broadcast_in_dim.63
  4.0 0.1 collective-permute-start
  4.1 0.7 fusion.17
  6.0 1.2 dynamic-slice
  7.9 0.9 dynamic-update-slice
  8.8 5.4 %all-reduce = s32[128]{0:T(128)S(1)} all-reduce(s32[128]{0:T(128)S(1)} %dynamic-update-slice), channel_id=1, replica_groups=mesh['grp'=4,'dev'=8] {'dev'}, use_global_device_ids=true, to_apply=%add | all-reduce | flops 128 | bytes 1024
  14.2 0.1 reshape.170
  14.9 0.0 collective-permute-done
  14.9 0.0 copy-start.3
  14.9 0.2 compare_reduce_fusion
  15.1 0.6 select_reduce_fusion.4
  17.7 0.0 collective-permute-done.2
  17.7 0.0 copy-done.3
  17.7 0.0 copy-start.1
  17.7 1.3 copy-done.1
  19.0 2.4 select_bitcast_fusion
  21.5 1.3 collective-permute-start.3
  24.6 0.0 copy-done.5
  24.7 0.3 convert_reduce_fusion
  24.9 0.6 multiply_add_fusion
  25.6 0.7 select_reduce_fusion.3
  28.1 2.9 fusion.13
  31.0 0.3 collective-permute-start.1
  31.3 0.7 fusion.21
  32.0 1.7 copy.23
  33.7 0.7 select_reduce_fusion.order_ref
  34.3 11.9 %collective-permute-done.1 = s32[28,1024]{1,0:T(8,128)S(1)} collective-permute-done((s32[28,1024]{1,0:T(8,128)}, s32[28,1024]{1,0:T(8,128)S(1)}, u32[]{:S(2)}, u32[]{:S(2)}) %collective-permute-start.1) | collective-permute-done | bytes 114720 | tf_op jit(solution)/shard_map/ppermute | solution.py:233
  46.3 0.5 slice.41
  47.4 0.7 slice_select_fusion.lists_ref
  48.0 0.0 collective-permute-done.3
  48.0 0.0 copy-done
  48.0 3.0 %bitcast_select_fusion.source_ref = bf16[1024,512]{1,0:T(8,128)(2,1)} fusion(bf16[1024,512]{1,0:T(8,128)(2,1)} %collective-permute-done.3, bf16[2,1024,512]{2,1,0:T(8,128)(2,1)} %copy-done.1, s32[]{:T(128)S(6)} %select_n.223, bf16[2,1024,512]{2,1,0:T(8,128)(2,1)S(1)} %bitcast.54, s32[]{:T(128)S(6)} %select_n.221, pred[]{:T(512)} %get-tuple-element.7, ...), kind=kLoop, calls=%fused_computation.15 | loop fusion | flops 1048576 | bytes 4194314 | tf_op jit(solution)/shard_map/jit(_where)/select_n | solution.py:235
  51.1 0.5 iota.48.fetch_ref
  51.6 74.7 %block.2 = bf16[1024,512]{1,0:T(8,128)(2,1)} custom-call(s32[16]{0:T(128)} %iota.48.fetch_ref, s32[16]{0:T(128)} %select_reduce_fusion.order_ref, bf16[1024,512]{1,0:T(8,128)(2,1)} %bitcast_select_fusion.source_ref, s32[27,1024]{1,0:T(8,128)} %slice_select_fusion.lists_ref, f32[512,27]{1,0:T(8,128)} %bitcast.58, bf16[512,512]{1,0:T(8,128)(2,1)} %mixing_ref.2, ...), custom_call_target="tpu_custom_call" | custom-call | flops 28991029248 | bytes 8388608 | tf_op jit(solution)/shard_map/block/pallas_call | solution.py:136
  126.3 6.3 %all-to-all-start = ((bf16[8,128,512]{2,1,0:T(8,128)(2,1)}), bf16[8,128,512]{2,1,0:T(8,128)(2,1)S(1)}, u32[]{:S(2)}, u32[]{:S(2)}) async-start(bf16[8,128,512]{2,1,0:T(8,128)(2,1)} %bitcast.55), calls=%async_computation | async-start | bytes 2097152 | tf_op jit(solution)/shard_map/all_to_all | solution.py:260
  132.6 0.1 add.108
  132.7 0.0 copy-done.4
  132.7 0.9 copy.24
  133.6 0.0 copy-done.6
  133.6 0.2 select_reduce_fusion.2.fetch_ref
  133.8 0.6 select_reduce_fusion.1.order_ref
  134.4 20.7 %all-to-all-done = bf16[8,128,512]{2,1,0:T(8,128)(2,1)S(1)} async-done(((bf16[8,128,512]{2,1,0:T(8,128)(2,1)}), bf16[8,128,512]{2,1,0:T(8,128)(2,1)S(1)}, u32[]{:S(2)}, u32[]{:S(2)}) %all-to-all-start) | async-done | bytes 1048608 | tf_op jit(solution)/shard_map/all_to_all | solution.py:260
  155.1 0.0 copy-done.8
  155.1 1.0 copy-done.2
  156.1 74.7 %block.3 = bf16[1024,512]{1,0:T(8,128)(2,1)} custom-call(s32[16]{0:T(128)} %copy-done.8, s32[16]{0:T(128)} %select_reduce_fusion.1.order_ref, bf16[1024,512]{1,0:T(8,128)(2,1)} %bitcast.56, s32[27,1024]{1,0:T(8,128)} %lists_ref.1, f32[512,27]{1,0:T(8,128)} %bitcast.59, bf16[512,512]{1,0:T(8,128)(2,1)} %mixing_ref.3, f32[1,512]{1,0:T(1,128)} %bitcast.61, ...), custom_call_target="tpu_custom_call" | custom-call | flops 28991029248 | bytes 8388608 | tf_op jit(solution)/shard_map/block/pallas_call | solution.py:136
  230.8 5.6 %all-to-all-start.1 = ((bf16[8,128,512]{2,1,0:T(8,128)(2,1)}), bf16[8,128,512]{2,1,0:T(8,128)(2,1)S(1)}, u32[]{:S(2)}, u32[]{:S(2)}) async-start(bf16[8,128,512]{2,1,0:T(8,128)(2,1)} %bitcast.57), calls=%async_computation.1 | async-start | bytes 2097152 | tf_op jit(solution)/shard_map/all_to_all | solution.py:260
  236.4 0.7 fusion.20
  237.1 21.9 %all-to-all-done.1 = bf16[8,128,512]{2,1,0:T(8,128)(2,1)S(1)} async-done(((bf16[8,128,512]{2,1,0:T(8,128)(2,1)}), bf16[8,128,512]{2,1,0:T(8,128)(2,1)S(1)}, u32[]{:S(2)}, u32[]{:S(2)}) %all-to-all-start.1) | async-done | bytes 1048608 | tf_op jit(solution)/shard_map/all_to_all | solution.py:260
  259.1 0.6 gather_fusion
  259.7 1.6 collective-permute-start.4
  261.3 21.5 %collective-permute-done.4 = bf16[1024,512]{1,0:T(8,128)(2,1)S(1)} collective-permute-done((bf16[1024,512]{1,0:T(8,128)(2,1)S(1)}, bf16[1024,512]{1,0:T(8,128)(2,1)S(1)}, u32[]{:S(2)}, u32[]{:S(2)}) %collective-permute-start.4) | collective-permute-done | bytes 1048608 | tf_op jit(solution)/shard_map/ppermute | solution.py:273
  282.8 1.5 pad_maximum_fusion
  284.3 2.6 collective-permute-start.5
  286.9 0.0 copy-done.7
  286.9 0.6 fusion.24
  291.2 0.6 fusion.23
  291.8 0.6 fusion.22
  292.4 0.0 collective-permute-done.5
  292.4 4.8 %fusion.3 = (bf16[1024,512]{1,0:T(8,128)(2,1)S(1)}, bf16[1024,512]{1,0:T(8,128)(2,1)S(1)}) fusion(s32[]{:T(128)S(6)} %select_n.235, bf16[1,1024,512]{2,1,0:T(8,128)(2,1)S(1)} %bitcast.46, bf16[1,1024,512]{2,1,0:T(8,128)(2,1)S(1)} %bitcast.49, bf16[2,1024,512]{2,1,0:T(8,128)(2,1)} %collective-permute-done.5, pred[]{:T(512)} %bitcast.2, pred[]{:T(512)} %bitcast.1, ...), kind=kLoop, calls=%fused_computation.10 | loop fusion | flops 3145728 | bytes 6291468 | tf_op jit(solution)/shard_map/jit(_where)/select_n | solution.py:279
  297.2 1.5 pad_maximum_fusion.1
  (16 shorter events, 0.1 us)
Async XLA Ops:
  0.0 17.7 %collective-permute-start.2 = (bf16[2,1024,512]{2,1,0:T(8,128)(2,1)}, bf16[2,1024,512]{2,1,0:T(8,128)(2,1)S(1)}, u32[]{:S(2)}, u32[]{:S(2)}) collective-permute-start(bf16[2,1024,512]{2,1,0:T(8,128)(2,1)} %bitcast.52), channel_id=1, source_target_pairs={{0,8},{8,0},{16,24},{24,16},{1,9},{9,1},{17,25},{25,17},{2,10},{10... | collective-permute-start | bytes 6291464 | tf_op jit(solution)/shard_map/ppermute | solution.py:207
  4.0 10.9 %collective-permute-start = (s32[2,28,1024]{2,1,0:T(8,128)S(1)}, s32[2,28,1024]{2,1,0:T(8,128)S(1)}, u32[]{:S(2)}, u32[]{:S(2)}) collective-permute-start(s32[2,28,1024]{2,1,0:T(8,128)S(1)} %pad_add_fusion), channel_id=1, source_target_pairs={{0,8},{8,0},{16,24},{24,16},{1,9},{9,1},{17,25},{25,17},{2,10},{10... | collective-permute-start | bytes 688136 | tf_op jit(solution)/shard_map/ppermute | solution.py:208
  14.2 10.5 %copy-start.5 = (s32[128]{0:T(128)}, s32[128]{0:T(128)S(1)}, u32[]{:S(2)}) copy-start(s32[128]{0:T(128)S(1)} %all-reduce) | copy-start | bytes 1540
  14.9 2.8 copy-start.3
  17.7 1.3 copy-start.1
  19.0 29.0 %copy-start = (bf16[2048,512]{1,0:T(8,128)(2,1)S(1)}, bf16[2048,512]{1,0:T(8,128)(2,1)}, u32[]{:S(2)}) copy-start(bf16[2048,512]{1,0:T(8,128)(2,1)} %param.16) | copy-start | bytes 6291460
  21.5 26.5 %collective-permute-start.3 = (bf16[1024,512]{1,0:T(8,128)(2,1)S(1)}, bf16[1024,512]{1,0:T(8,128)(2,1)}, u32[]{:S(2)}, u32[]{:S(2)}) collective-permute-start(bf16[1024,512]{1,0:T(8,128)(2,1)S(1)} %select_bitcast_fusion), channel_id=1, source_target_pairs={{0,16},{8,24},{16,0},{24,8},{1,17},{9,25},{17,1},{25,9},{2,18},{10... | collective-permute-start | bytes 3145736 | tf_op jit(solution)/shard_map/ppermute | solution.py:232
  31.0 15.2 %collective-permute-start.1 = (s32[28,1024]{1,0:T(8,128)}, s32[28,1024]{1,0:T(8,128)S(1)}, u32[]{:S(2)}, u32[]{:S(2)}) collective-permute-start(s32[28,1024]{1,0:T(8,128)} %get-tuple-element.15), channel_id=1, source_target_pairs={{0,16},{8,24},{16,0},{24,8},{1,17},{9,25},{17,1},{25,9},{2,18},{10... | collective-permute-start | bytes 344072 | tf_op jit(solution)/shard_map/ppermute | solution.py:233
  126.3 6.4 %copy-start.4 = (f32[27,512]{1,0:T(8,128)S(1)}, f32[27,512]{1,0:T(8,128)}, u32[]{:S(2)}) copy-start(f32[27,512]{1,0:T(8,128)} %param.27) | copy-start | bytes 165892
  126.3 7.3 %copy-start.6 = (s32[128]{0:T(128)S(1)}, s32[128]{0:T(128)}, u32[]{:S(2)}) copy-start(s32[128]{0:T(128)} %copy-done.5) | copy-start | bytes 1540
  126.3 28.8 %all-to-all-start = ((bf16[8,128,512]{2,1,0:T(8,128)(2,1)}), bf16[8,128,512]{2,1,0:T(8,128)(2,1)S(1)}, u32[]{:S(2)}, u32[]{:S(2)}) async-start(bf16[8,128,512]{2,1,0:T(8,128)(2,1)} %bitcast.55), calls=%async_computation | async-start | bytes 2097152 | tf_op jit(solution)/shard_map/all_to_all | solution.py:260
  133.8 21.4 %copy-start.8 = (s32[16]{0:T(128)}, s32[16]{0:T(128)S(1)}, u32[]{:S(2)}) copy-start(s32[16]{0:T(128)S(1)} %select_reduce_fusion.2.fetch_ref) | copy-start | bytes 196
  155.1 1.0 copy-start.2
  230.8 28.2 %all-to-all-start.1 = ((bf16[8,128,512]{2,1,0:T(8,128)(2,1)}), bf16[8,128,512]{2,1,0:T(8,128)(2,1)S(1)}, u32[]{:S(2)}, u32[]{:S(2)}) async-start(bf16[8,128,512]{2,1,0:T(8,128)(2,1)} %bitcast.57), calls=%async_computation.1 | async-start | bytes 2097152 | tf_op jit(solution)/shard_map/all_to_all | solution.py:260
  259.7 23.1 %collective-permute-start.4 = (bf16[1024,512]{1,0:T(8,128)(2,1)S(1)}, bf16[1024,512]{1,0:T(8,128)(2,1)S(1)}, u32[]{:S(2)}, u32[]{:S(2)}) collective-permute-start(bf16[1024,512]{1,0:T(8,128)(2,1)S(1)} %bitcast.44), channel_id=1, source_target_pairs={{0,16},{8,24},{16,0},{24,8},{1,17},{9,25},{17,1},{25,9},{2,18},{10... | collective-permute-start | bytes 3145736 | tf_op jit(solution)/shard_map/ppermute | solution.py:273
  282.8 4.1 %copy-start.7 = (s32[2]{0:T(128)S(1)}, s32[2]{0:T(128)}, u32[]{:S(2)}) copy-start(s32[2]{0:T(128)} %param.18) | copy-start | bytes 28
  284.3 8.1 %collective-permute-start.5 = (bf16[2,1024,512]{2,1,0:T(8,128)(2,1)}, bf16[2,1024,512]{2,1,0:T(8,128)(2,1)}, u32[]{:S(2)}, u32[]{:S(2)}) collective-permute-start(bf16[2,1024,512]{2,1,0:T(8,128)(2,1)} %pad_maximum_fusion), channel_id=1, source_target_pairs={{0,8},{8,0},{16,24},{24,16},{1,9},{9,1},{17,25},{25,17},{2,10},{10... | collective-permute-start | bytes 6291464 | tf_op jit(solution)/shard_map/ppermute | solution.py:275
where the time goes:
time: 302 us; the launch traced here: 299 us
  Pallas kernels  149 us (49%)
  waiting for transfers between devices  76.1 us (25%)
  other arithmetic  23.4 us (8%)
  starting transfers between devices  18.4 us (6%)
  between operations  13.3 us (4%)
  local copies, waits for them, and re-layouts  12.5 us (4%)
  blocking collectives  5.42 us (2%)
    pallas_call x2, Pallas kernels, run_block(): pl.pallas_call(block_kernel, out_shape=jax.ShapeDtypeStruct((order.shape[...  149 us
    all_to_all x2, waiting for transfers between devices, body(): lax.all_to_all(a, 'dev', split_axis=0, concat_axis=0, tiled=True)  42.7 us
    ppermute x1, waiting for transfers between devices, body(): gathered.append(lax.ppermute(finished, 'grp', over))  21.5 us
    ppermute x1, waiting for transfers between devices, body(): stamps_in = lax.ppermute(stamps_out, 'grp', over)  11.9 us
    all_to_all x2, starting transfers between devices, body(): lax.all_to_all(a, 'dev', split_axis=0, concat_axis=0, tiled=True)  11.9 us
    unnamed x23, local copies, waits for them, and re-layouts  6.98 us
  transfers between devices with their start and end apart: 8, of which 4 were waited for; matrix products, arithmetic and copies ran while one was open for 6% of the time, Pallas kernels for 0%

commit v1 on v0

--- a/solution.py
+++ b/solution.py
@@ -15,14 +15,18 @@
 CHUNK = 256
 EPSILON = 1e-05
 ONES = 16
+PRODUCTS = 12
+STEP = 3
 
 
 def block_kernel(
     fetch_ref,
     order_ref,
+    near_ref,
     source_ref,
     lists_ref,
     depth_ref,
+    turned_ref,
     mixing_ref,
     gain_ref,
     qkv_ref,
@@ -30,6 +34,9 @@
     out_ref,
     x_ref,
     xt_ref,
+    fine_ref,
+    slim_ref,
+    sums_ref,
     wide_ref,
     acc_ref,
     code_ref,
@@ -41,38 +48,61 @@
     result_ref,
 ):
     rows, width = x_ref.shape
-    fanout = depth_ref.shape[1]
+    fanout = depth_ref.shape[0]
     in_blocks = fetch_ref.shape[0]
     out_blocks = order_ref.shape[0]
     piece = rows // in_blocks
     chunks = rows // CHUNK
+    lanes = 128
+    parts = width // lanes
     for b in range(in_blocks):
         x_ref[pl.ds(b * piece, piece), :] = source_ref[
             pl.ds(pl.multiple_of(fetch_ref[b] * piece, piece), piece), :
         ]
     xt_ref[...] = x_ref[...].T
-    for j in range(fanout):
-        wide_ref[j] = jnp.broadcast_to(depth_ref[:, j : j + 1], (width, 128))
-    places = lax.broadcasted_iota(jnp.int32, (rows, CHUNK), 0).astype(jnp.int16)
+    for c in range(parts):
+        fine_ref[pl.ds(c, rows, stride=parts), :] = x_ref[:, c * lanes : (c + 1) * lanes].astype(
+            jnp.float32
+        )
+        slim_ref[pl.ds(c, fanout, stride=parts), :] = depth_ref[:, c * lanes : (c + 1) * lanes]
+    for j in range(PRODUCTS):
+        wide_ref[j] = jnp.broadcast_to(turned_ref[:, j : j + 1], (width, lanes))
+    places = (lax.broadcasted_iota(jnp.int32, (rows, CHUNK), 0) * parts).astype(jnp.int16)
+    one, nil = jnp.bfloat16(1), jnp.bfloat16(0)
+    turns = PRODUCTS // STEP
+    points = CHUNK // turns
 
     @pl.loop(0, chunks)
     def _(c):
         at = pl.multiple_of(c * CHUNK, CHUNK)
         acc_ref[...] = jnp.zeros_like(acc_ref)
 
-        @pl.loop(0, fanout, step=3)
-        def _(j0):
+        @pl.loop(0, turns)
+        def _(t):
             total = acc_ref[...]
-            for dj in range(3):
-                j = j0 + dj
+            for dj in range(STEP):
+                j = t * STEP + dj
                 row = lists_ref[pl.ds(j, 1), pl.ds(at, CHUNK)].astype(jnp.int16)
-                hot = jnp.where(places == row, 1.0, 0.0).astype(jnp.bfloat16)
+                hot = jnp.where(places == row, one, nil)
                 got = jnp.dot(xt_ref[...], hot, preferred_element_type=jnp.float32)
                 weight = wide_ref[j]
-                total = total + got * jnp.concatenate([weight] * (CHUNK // 128), axis=1)
+                total = total + got * jnp.concatenate([weight] * (CHUNK // lanes), axis=1)
             acc_ref[...] = total
-
-        code_ref[pl.ds(at, CHUNK), :] = acc_ref[...].T.astype(jnp.bfloat16)
+            first = t * points
+            weights = [slim_ref[pl.ds(j * parts, parts), :] for j in range(PRODUCTS, fanout)]
+            for p in range(points):
+                total = None
+                for j in range(PRODUCTS, fanout):
+                    line = pl.multiple_of(near_ref[j, at + first + p], parts)
+                    term = fine_ref[pl.ds(line, parts), :] * weights[j - PRODUCTS]
+                    total = term if total is None else total + term
+                sums_ref[pl.ds(pl.multiple_of((first + p) * parts, parts), parts), :] = total
+
+        for i in range(parts):
+            code_ref[pl.ds(at, CHUNK), i * lanes : (i + 1) * lanes] = (
+                acc_ref[i * lanes : (i + 1) * lanes, :].T
+                + sums_ref[pl.ds(i, CHUNK, stride=parts), :]
+            ).astype(jnp.bfloat16)
 
     gain = gain_ref[...]
     scale = HEAD_DIM**-0.5 * math.log2(math.e)
@@ -100,20 +130,28 @@
     @pl.loop(0, chunks)
     def _(c):
         here = pl.ds(pl.multiple_of(c * CHUNK, CHUNK), CHUNK)
-        for h in range(HEADS):
+
+        def scored(h):
             pair = h // 2
             zero = jnp.zeros((HEAD_DIM, CHUNK), jnp.bfloat16)
             query = qt_ref[pl.ds(h * HEAD_DIM, HEAD_DIM), here]
             padded = jnp.concatenate([query, zero] if h % 2 == 0 else [zero, query], axis=0)
-            scores = jnp.dot(
-                k_ref[:, pair * 128 : (pair + 1) * 128], padded, preferred_element_type=jnp.float32
+            return jnp.dot(
+                k_ref[:, pair * lanes : (pair + 1) * lanes],
+                padded,
+                preferred_element_type=jnp.float32,
             )
+
+        scores = scored(0)
+        for h in range(HEADS):
+            following = scored(h + 1) if h + 1 < HEADS else None
             peak = jnp.max(scores, axis=0, keepdims=True)
             powers = jnp.exp2(scores - peak).astype(jnp.bfloat16)
             mixed = jnp.dot(vt_ref[h], powers, preferred_element_type=jnp.float32)
             mixed_ref[pl.ds(h * HEAD_DIM, HEAD_DIM), :] = (
                 mixed[:HEAD_DIM] / mixed[HEAD_DIM : HEAD_DIM + 1]
             )
+            scores = following
         mixed = mixed_ref[...].T.astype(jnp.bfloat16)
         result_ref[here, :] = (
             updated_ref[here, :]
@@ -126,22 +164,26 @@
         ]
 
 
-def run_block(source, lists, params, fetch, order, rows):
+def run_block(source, lines, params, fetch, order, rows):
     depth, mixing, gain, w_qkv, w_out = params
     width = source.shape[1]
-    fanout = lists.shape[0]
+    fanout = lines.shape[0]
     piece = rows // fetch.shape[0]
+    parts = width // 128
     vmem = pl.BlockSpec(memory_space=pltpu.VMEM)
     smem = pl.BlockSpec(memory_space=pltpu.SMEM)
     return pl.pallas_call(
         block_kernel,
         out_shape=jax.ShapeDtypeStruct((order.shape[0] * piece, width), jnp.bfloat16),
-        in_specs=[smem, smem] + [vmem] * 7,
+        in_specs=[smem] * 3 + [vmem] * 8,
         out_specs=vmem,
         scratch_shapes=[
             pltpu.VMEM((rows, width), jnp.bfloat16),
             pltpu.VMEM((width, rows), jnp.bfloat16),
-            pltpu.VMEM((fanout, width, 128), jnp.float32),
+            pltpu.VMEM((rows * parts, 128), jnp.float32),
+            pltpu.VMEM((fanout * parts, 128), jnp.float32),
+            pltpu.VMEM((CHUNK * parts, 128), jnp.float32),
+            pltpu.VMEM((PRODUCTS, width, 128), jnp.float32),
             pltpu.VMEM((width, CHUNK), jnp.float32),
             pltpu.VMEM((rows, width), jnp.bfloat16),
             pltpu.VMEM((rows, width), jnp.float32),
@@ -156,7 +198,19 @@
             flops=2 * fanout * rows * rows * width, bytes_accessed=8 << 20, transcendentals=8 << 20
         ),
         name="block",
-    )(fetch, order, source, lists, depth.T, mixing, gain.reshape(1, width), w_qkv, w_out)
+    )(
+        fetch,
+        order,
+        lines,
+        source,
+        lines,
+        depth,
+        depth.T,
+        mixing,
+        gain.reshape(1, width),
+        w_qkv,
+        w_out,
+    )
 
 
 def body(
@@ -256,10 +310,10 @@
     ).astype(jnp.int32)
 
     straight = jnp.arange(block_count, dtype=jnp.int32)
-    outgoing = run_block(points, stamps[:fanout], first_params, straight, order, rows)
+    outgoing = run_block(points, stamps[:fanout] * (width // 128), first_params, straight, order, rows)
     swap = lambda a: lax.all_to_all(a, "dev", split_axis=0, concat_axis=0, tiled=True)
     incoming = swap(outgoing)
-    backward = run_block(incoming, neighbors_second, second_params, fetch, back, rows)
+    backward = run_block(incoming, neighbors_second * (width // 128), second_params, fetch, back, rows)
     returned = swap(backward).reshape(slots, piece, width)
     finished = returned[place].reshape(rows, width)
 

time: 302 us -> 265 us (0.88)
  Pallas kernels: 149 us -> 113 us
    pallas_call x2, Pallas kernels: 149 us -> 113 us  [run_block(): pl.pallas_call(block_kernel, out_shape=jax.ShapeDtypeStruct((order.shape[...]
    unnamed x23 -> x25, local copies, waits for them, and re-layouts: 6.98 us -> 6.98 us
  transfers between devices with their start and end apart: 8 -> 8, of which waited for: 4 -> 4; matrix products, arithmetic and copies ran while one was open for 6% -> 8% of each run, Pallas kernels for 0% -> 0%
where the time goes in v1:
time: 265 us; the launch traced here: 262 us
  Pallas kernels  113 us (43%)
  waiting for transfers between devices  75.6 us (29%)
  other arithmetic  24.1 us (9%)
  starting transfers between devices  18.4 us (7%)
  between operations  13.3 us (5%)
  local copies, waits for them, and re-layouts  12.5 us (5%)
  blocking collectives  5.42 us (2%)
    pallas_call x2, Pallas kernels, run_block(): pl.pallas_call(block_kernel, out_shape=jax.ShapeDtypeStruct((order.shape[...  113 us
    all_to_all x2, waiting for transfers between devices, body(): lax.all_to_all(a, 'dev', split_axis=0, concat_axis=0, tiled=True)  42 us
    ppermute x1, waiting for transfers between devices, body(): gathered.append(lax.ppermute(finished, 'grp', over))  21.7 us
    all_to_all x2, starting transfers between devices, body(): lax.all_to_all(a, 'dev', split_axis=0, concat_axis=0, tiled=True)  12.2 us
    ppermute x1, waiting for transfers between devices, body(): stamps_in = lax.ppermute(stamps_out, 'grp', over)  11.9 us
    unnamed x25, local copies, waits for them, and re-layouts  6.98 us
    unnamed x1, blocking collectives  5.42 us
    select_n x2, other arithmetic, candidate(): jnp.where(ours, lax.dynamic_index_in_dim(a, at_here, 0, keepdims=False),...  5.37 us
  transfers between devices with their start and end apart: 8, of which 4 were waited for; matrix products, arithmetic and copies ran while one was open for 8% of the time, Pallas kernels for 0%

profile of v1, /device:TPU:25, one launch (start us, length us, event | category | flops | bytes accessed | tf_op | source)
XLA Modules:
  0.0 262.2 jit_solution(2536397605111956947)
XLA Ops:
  0.0 0.7 collective-permute-start.2
  1.3 1.1 reshape.171
  2.5 0.1 copy.26
  2.6 1.3 compare_reduce_fusion.3
  3.9 0.1 broadcast_in_dim.63
  4.0 0.1 collective-permute-start
  4.1 0.7 fusion.17
  6.0 1.2 dynamic-slice
  7.9 0.9 dynamic-update-slice
  8.8 5.4 %all-reduce = s32[128]{0:T(128)S(1)} all-reduce(s32[128]{0:T(128)S(1)} %dynamic-update-slice), channel_id=1, replica_groups=mesh['grp'=4,'dev'=8] {'dev'}, use_global_device_ids=true, to_apply=%add | all-reduce | flops 128 | bytes 1024
  14.2 0.1 reshape.170
  14.9 0.0 collective-permute-done
  14.9 0.0 copy-start.3
  14.9 0.2 compare_reduce_fusion.1
  15.1 0.6 select_reduce_fusion.4
  17.7 0.0 collective-permute-done.2
  17.7 0.0 copy-done.3
  17.7 0.0 copy-start.1
  17.7 1.3 copy-done.1
  19.0 2.4 select_bitcast_fusion
  21.5 1.3 collective-permute-start.3
  24.7 0.0 copy-done.6
  24.7 0.3 convert_reduce_fusion
  24.9 0.6 multiply_add_fusion
  25.6 0.7 select_reduce_fusion.3
  28.1 2.9 %fusion.10 = (s32[28,1024]{1,0:T(8,128)}, s32[28,1024]{1,0:T(8,128)S(1)}) fusion(s32[]{:T(128)S(6)} %select_n.210, s32[2,27,1024]{2,1,0:T(8,128)S(1)} %bitcast.51, s32[2,1,1024]{2,1,0:T(1,128)S(1)} %broadcast_in_dim.63, s32[2,28,1024]{2,1,0:T(8,128)} %copy-done.3, s32[]{:T(128)S(6)} %select_n.212, pred[]{:T(512)} %get-tuple-element.7, s32[]{:T(128)S(6)} %select_n.220, ...), kind=kLoop, calls=%fused_computation.25 | loop fusion | flops 114688 | bytes 688146 | tf_op jit(solution)/shard_map/jit(_where)/select_n | solution.py:270
  31.0 0.2 collective-permute-start.1
  31.3 0.7 fusion.22
  32.0 1.7 copy.23
  33.7 0.7 select_reduce_fusion.order_ref
  34.3 11.9 %collective-permute-done.1 = s32[28,1024]{1,0:T(8,128)S(1)} collective-permute-done((s32[28,1024]{1,0:T(8,128)}, s32[28,1024]{1,0:T(8,128)S(1)}, u32[]{:S(2)}, u32[]{:S(2)}) %collective-permute-start.1) | collective-permute-done | bytes 114720 | tf_op jit(solution)/shard_map/ppermute | solution.py:287
  46.3 0.5 slice.41
  47.4 0.7 fusion.14.near_ref.lists_ref
  48.0 0.0 collective-permute-done.3
  48.0 0.0 copy-done
  48.0 3.0 %bitcast_select_fusion.source_ref = bf16[1024,512]{1,0:T(8,128)(2,1)} fusion(bf16[1024,512]{1,0:T(8,128)(2,1)} %collective-permute-done.3, bf16[2,1024,512]{2,1,0:T(8,128)(2,1)} %copy-done.1, s32[]{:T(128)S(6)} %select_n.220, bf16[2,1024,512]{2,1,0:T(8,128)(2,1)S(1)} %bitcast.54, s32[]{:T(128)S(6)} %select_n.218, pred[]{:T(512)} %get-tuple-element.8, ...), kind=kLoop, calls=%fused_computation.15 | loop fusion | flops 1048576 | bytes 4194314 | tf_op jit(solution)/shard_map/jit(_where)/select_n | solution.py:289
  51.1 0.5 iota.48.fetch_ref
  51.6 56.3 %block.2 = bf16[1024,512]{1,0:T(8,128)(2,1)} custom-call(s32[16]{0:T(128)} %iota.48.fetch_ref, s32[16]{0:T(128)} %select_reduce_fusion.order_ref, s32[27,1024]{1,0:T(8,128)} %fusion.14.near_ref.lists_ref, bf16[1024,512]{1,0:T(8,128)(2,1)} %bitcast_select_fusion.source_ref, s32[27,1024]{1,0:T(8,128)} %fusion.14.near_ref.lists_ref, f32[27,512]{1,0:T(8,128)} %depth_ref.2, ...), custom_call_target="tpu_custom_call" | custom-call | flops 28991029248 | bytes 8388608 | tf_op jit(solution)/shard_map/block/pallas_call | solution.py:175
  107.9 6.6 %all-to-all-start = ((bf16[8,128,512]{2,1,0:T(8,128)(2,1)}), bf16[8,128,512]{2,1,0:T(8,128)(2,1)S(1)}, u32[]{:S(2)}, u32[]{:S(2)}) async-start(bf16[8,128,512]{2,1,0:T(8,128)(2,1)} %bitcast.55), calls=%async_computation | async-start | bytes 2097152 | tf_op jit(solution)/shard_map/all_to_all | solution.py:314
  114.6 0.1 add.108
  114.7 0.0 copy-done.5
  114.7 0.9 copy.24
  115.5 0.0 copy-done.7
  115.5 0.2 select_reduce_fusion.2.fetch_ref
  115.7 0.7 select_reduce_fusion.1.order_ref
  116.4 0.7 broadcast_multiply_fusion.near_ref.lists_ref
  117.1 20.1 %all-to-all-done = bf16[8,128,512]{2,1,0:T(8,128)(2,1)S(1)} async-done(((bf16[8,128,512]{2,1,0:T(8,128)(2,1)}), bf16[8,128,512]{2,1,0:T(8,128)(2,1)S(1)}, u32[]{:S(2)}, u32[]{:S(2)}) %all-to-all-start) | async-done | bytes 1048608 | tf_op jit(solution)/shard_map/all_to_all | solution.py:314
  137.2 0.0 copy-done.9
  137.2 1.0 copy-done.2
  138.1 56.4 %block.3 = bf16[1024,512]{1,0:T(8,128)(2,1)} custom-call(s32[16]{0:T(128)} %copy-done.9, s32[16]{0:T(128)} %select_reduce_fusion.1.order_ref, s32[27,1024]{1,0:T(8,128)} %broadcast_multiply_fusion.near_ref.lists_ref, bf16[1024,512]{1,0:T(8,128)(2,1)} %bitcast.56, s32[27,1024]{1,0:T(8,128)} %broadcast_multiply_fusion.near_ref.lists_ref, f32[27,512]{1,0:T(8,128)} %depth_ref.3, ...), custom_call_target="tpu_custom_call" | custom-call | flops 28991029248 | bytes 8388608 | tf_op jit(solution)/shard_map/block/pallas_call | solution.py:175
  194.5 5.5 %all-to-all-start.1 = ((bf16[8,128,512]{2,1,0:T(8,128)(2,1)}), bf16[8,128,512]{2,1,0:T(8,128)(2,1)S(1)}, u32[]{:S(2)}, u32[]{:S(2)}) async-start(bf16[8,128,512]{2,1,0:T(8,128)(2,1)} %bitcast.57), calls=%async_computation.1 | async-start | bytes 2097152 | tf_op jit(solution)/shard_map/all_to_all | solution.py:314
  200.1 0.7 fusion.21
  200.7 21.9 %all-to-all-done.1 = bf16[8,128,512]{2,1,0:T(8,128)(2,1)S(1)} async-done(((bf16[8,128,512]{2,1,0:T(8,128)(2,1)}), bf16[8,128,512]{2,1,0:T(8,128)(2,1)S(1)}, u32[]{:S(2)}, u32[]{:S(2)}) %all-to-all-start.1) | async-done | bytes 1048608 | tf_op jit(solution)/shard_map/all_to_all | solution.py:314
  222.7 0.6 gather_fusion
  223.3 1.3 collective-permute-start.4
  224.6 21.7 %collective-permute-done.4 = bf16[1024,512]{1,0:T(8,128)(2,1)S(1)} collective-permute-done((bf16[1024,512]{1,0:T(8,128)(2,1)S(1)}, bf16[1024,512]{1,0:T(8,128)(2,1)S(1)}, u32[]{:S(2)}, u32[]{:S(2)}) %collective-permute-start.4) | collective-permute-done | bytes 1048608 | tf_op jit(solution)/shard_map/ppermute | solution.py:327
  246.3 1.5 pad_maximum_fusion
  247.8 2.7 %collective-permute-start.5 = (bf16[2,1024,512]{2,1,0:T(8,128)(2,1)}, bf16[2,1024,512]{2,1,0:T(8,128)(2,1)}, u32[]{:S(2)}, u32[]{:S(2)}) collective-permute-start(bf16[2,1024,512]{2,1,0:T(8,128)(2,1)} %pad_maximum_fusion), channel_id=1, source_target_pairs={{0,8},{8,0},{16,24},{24,16},{1,9},{9,1},{17,25},{25,17},{2,10},{10... | collective-permute-start | bytes 6291464 | tf_op jit(solution)/shard_map/ppermute | solution.py:329
  250.5 0.6 fusion.25
  254.8 0.6 fusion.24
  255.4 0.6 fusion.23
  256.0 0.0 collective-permute-done.5
  256.0 4.8 %fusion.3 = (bf16[1024,512]{1,0:T(8,128)(2,1)S(1)}, bf16[1024,512]{1,0:T(8,128)(2,1)S(1)}) fusion(s32[]{:T(128)S(6)} %select_n.235, bf16[1,1024,512]{2,1,0:T(8,128)(2,1)S(1)} %bitcast.46, bf16[1,1024,512]{2,1,0:T(8,128)(2,1)S(1)} %bitcast.49, bf16[2,1024,512]{2,1,0:T(8,128)(2,1)} %collective-permute-done.5, pred[]{:T(512)} %bitcast.2, pred[]{:T(512)} %bitcast.1, ...), kind=kLoop, calls=%fused_computation.10 | loop fusion | flops 3145728 | bytes 6291468 | tf_op jit(solution)/shard_map/jit(_where)/select_n | solution.py:333
  260.8 1.5 pad_maximum_fusion.1
  (19 shorter events, 0.1 us)
Async XLA Ops:
  0.0 17.7 %collective-permute-start.2 = (bf16[2,1024,512]{2,1,0:T(8,128)(2,1)}, bf16[2,1024,512]{2,1,0:T(8,128)(2,1)S(1)}, u32[]{:S(2)}, u32[]{:S(2)}) collective-permute-start(bf16[2,1024,512]{2,1,0:T(8,128)(2,1)} %bitcast.52), channel_id=1, source_target_pairs={{0,8},{8,0},{16,24},{24,16},{1,9},{9,1},{17,25},{25,17},{2,10},{10... | collective-permute-start | bytes 6291464 | tf_op jit(solution)/shard_map/ppermute | solution.py:261
  4.0 10.9 %collective-permute-start = (s32[2,28,1024]{2,1,0:T(8,128)S(1)}, s32[2,28,1024]{2,1,0:T(8,128)S(1)}, u32[]{:S(2)}, u32[]{:S(2)}) collective-permute-start(s32[2,28,1024]{2,1,0:T(8,128)S(1)} %pad_add_fusion), channel_id=1, source_target_pairs={{0,8},{8,0},{16,24},{24,16},{1,9},{9,1},{17,25},{25,17},{2,10},{10... | collective-permute-start | bytes 688136 | tf_op jit(solution)/shard_map/ppermute | solution.py:262
  14.2 10.5 %copy-start.6 = (s32[128]{0:T(128)}, s32[128]{0:T(128)S(1)}, u32[]{:S(2)}) copy-start(s32[128]{0:T(128)S(1)} %all-reduce) | copy-start | bytes 1540
  14.9 2.8 %copy-start.3 = (s32[2,28,1024]{2,1,0:T(8,128)}, s32[2,28,1024]{2,1,0:T(8,128)S(1)}, u32[]{:S(2)}) copy-start(s32[2,28,1024]{2,1,0:T(8,128)S(1)} %collective-permute-done) | copy-start | bytes 688132
  17.7 1.3 copy-start.1
  19.0 29.0 %copy-start = (bf16[2048,512]{1,0:T(8,128)(2,1)S(1)}, bf16[2048,512]{1,0:T(8,128)(2,1)}, u32[]{:S(2)}) copy-start(bf16[2048,512]{1,0:T(8,128)(2,1)} %param.16) | copy-start | bytes 6291460
  21.5 26.5 %collective-permute-start.3 = (bf16[1024,512]{1,0:T(8,128)(2,1)S(1)}, bf16[1024,512]{1,0:T(8,128)(2,1)}, u32[]{:S(2)}, u32[]{:S(2)}) collective-permute-start(bf16[1024,512]{1,0:T(8,128)(2,1)S(1)} %select_bitcast_fusion), channel_id=1, source_target_pairs={{0,16},{8,24},{16,0},{24,8},{1,17},{9,25},{17,1},{25,9},{2,18},{10... | collective-permute-start | bytes 3145736 | tf_op jit(solution)/shard_map/ppermute | solution.py:286
  31.0 15.2 %collective-permute-start.1 = (s32[28,1024]{1,0:T(8,128)}, s32[28,1024]{1,0:T(8,128)S(1)}, u32[]{:S(2)}, u32[]{:S(2)}) collective-permute-start(s32[28,1024]{1,0:T(8,128)} %get-tuple-element.14), channel_id=1, source_target_pairs={{0,16},{8,24},{16,0},{24,8},{1,17},{9,25},{17,1},{25,9},{2,18},{10... | collective-permute-start | bytes 344072 | tf_op jit(solution)/shard_map/ppermute | solution.py:287
  107.9 6.7 %copy-start.5 = (f32[27,512]{1,0:T(8,128)S(1)}, f32[27,512]{1,0:T(8,128)}, u32[]{:S(2)}) copy-start(f32[27,512]{1,0:T(8,128)} %depth_ref.3) | copy-start | bytes 165892
  107.9 7.6 %copy-start.7 = (s32[128]{0:T(128)S(1)}, s32[128]{0:T(128)}, u32[]{:S(2)}) copy-start(s32[128]{0:T(128)} %copy-done.6) | copy-start | bytes 1540
  107.9 8.5 %copy-start.4 = (s32[27,1024]{1,0:T(8,128)S(1)}, s32[27,1024]{1,0:T(8,128)}, u32[]{:S(2)}) copy-start(s32[27,1024]{1,0:T(8,128)} %param.21) | copy-start | bytes 331780
  107.9 29.2 %all-to-all-start = ((bf16[8,128,512]{2,1,0:T(8,128)(2,1)}), bf16[8,128,512]{2,1,0:T(8,128)(2,1)S(1)}, u32[]{:S(2)}, u32[]{:S(2)}) async-start(bf16[8,128,512]{2,1,0:T(8,128)(2,1)} %bitcast.55), calls=%async_computation | async-start | bytes 2097152 | tf_op jit(solution)/shard_map/all_to_all | solution.py:314
  115.7 21.4 %copy-start.9 = (s32[16]{0:T(128)}, s32[16]{0:T(128)S(1)}, u32[]{:S(2)}) copy-start(s32[16]{0:T(128)S(1)} %select_reduce_fusion.2.fetch_ref) | copy-start | bytes 196
  137.2 1.0 copy-start.2
  194.5 28.2 %all-to-all-start.1 = ((bf16[8,128,512]{2,1,0:T(8,128)(2,1)}), bf16[8,128,512]{2,1,0:T(8,128)(2,1)S(1)}, u32[]{:S(2)}, u32[]{:S(2)}) async-start(bf16[8,128,512]{2,1,0:T(8,128)(2,1)} %bitcast.57), calls=%async_computation.1 | async-start | bytes 2097152 | tf_op jit(solution)/shard_map/all_to_all | solution.py:314
  223.3 23.0 %collective-permute-start.4 = (bf16[1024,512]{1,0:T(8,128)(2,1)S(1)}, bf16[1024,512]{1,0:T(8,128)(2,1)S(1)}, u32[]{:S(2)}, u32[]{:S(2)}) collective-permute-start(bf16[1024,512]{1,0:T(8,128)(2,1)S(1)} %bitcast.44), channel_id=1, source_target_pairs={{0,16},{8,24},{16,0},{24,8},{1,17},{9,25},{17,1},{25,9},{2,18},{10... | collective-permute-start | bytes 3145736 | tf_op jit(solution)/shard_map/ppermute | solution.py:327
  246.3 4.2 %copy-start.8 = (s32[2]{0:T(128)S(1)}, s32[2]{0:T(128)}, u32[]{:S(2)}) copy-start(s32[2]{0:T(128)} %param.18) | copy-start | bytes 28
  247.8 8.2 %collective-permute-start.5 = (bf16[2,1024,512]{2,1,0:T(8,128)(2,1)}, bf16[2,1024,512]{2,1,0:T(8,128)(2,1)}, u32[]{:S(2)}, u32[]{:S(2)}) collective-permute-start(bf16[2,1024,512]{2,1,0:T(8,128)(2,1)} %pad_maximum_fusion), channel_id=1, source_target_pairs={{0,8},{8,0},{16,24},{24,16},{1,9},{9,1},{17,25},{25,17},{2,10},{10... | collective-permute-start | bytes 6291464 | tf_op jit(solution)/shard_map/ppermute | solution.py:329

commit v2 on v1

--- a/solution.py
+++ b/solution.py
@@ -17,9 +17,215 @@
 ONES = 16
 PRODUCTS = 12
 STEP = 3
-
-
-def block_kernel(
+LIMIT = 56 * 1024 * 1024
+
+
+MESH = pl.DeviceIdType.MESH
+
+
+def around(size, at, step):
+    return lax.rem(at + step + size, size)
+
+
+def greet(peers):
+    barrier = pltpu.get_barrier_semaphore()
+    for peer in peers:
+        pl.semaphore_signal(barrier, inc=1, device_id=peer, device_id_type=MESH)
+    return lambda: pl.semaphore_wait(barrier, len(peers))
+
+
+def neighbours_of(groups, owners):
+    me, mine = lax.axis_index("grp"), lax.axis_index("dev")
+    chip, core = me // CORES, lax.rem(me, CORES)
+    mate = (chip * CORES + 1 - core, mine)
+    over = ((1 - chip) * CORES + core, mine)
+    slant = ((1 - chip) * CORES + 1 - core, mine)
+    return mate, over, slant
+
+
+def owners_kernel(
+    owners,
+    points_ref,
+    lists_ref,
+    meta_ref,
+    points_out,
+    lists_out,
+    metas_out,
+    mate_points,
+    mate_lists,
+    out_points,
+    out_lists,
+    in_points,
+    in_lists,
+    metas_ref,
+    meta_send,
+    meta_recv,
+    mate_send,
+    mate_recv,
+    over_send,
+    over_recv,
+):
+    me, mine = lax.axis_index("grp"), lax.axis_index("dev")
+    rows = points_out.shape[0]
+    half = rows // 2
+    mate, over, slant = neighbours_of(4, owners)
+    column = [mate, over, slant]
+    line = [(me, around(owners, mine, k)) for k in range(1, owners)]
+    peers = column + line
+    entered = greet(peers)
+    entered()
+
+    def meta_copy(i, slot):
+        return pltpu.make_async_remote_copy(
+            meta_ref,
+            metas_ref.at[slot],
+            meta_send.at[i],
+            meta_recv.at[i],
+            device_id=peers[i],
+            device_id_type=MESH,
+        )
+
+    count = len(peers)
+    metas = [meta_copy(i, i if i < 3 else i + 1) for i in range(count)]
+    for copy in metas:
+        copy.start()
+    metas_ref[3] = meta_ref[...]
+
+    def mate_copy(i):
+        slot, part = i % 2, i // 2
+        span = pl.ds(slot * rows + part * half, half)
+        return pltpu.make_async_remote_copy(
+            points_ref.at[span],
+            mate_points.at[span],
+            mate_send.at[i],
+            mate_recv.at[i],
+            device_id=mate,
+            device_id_type=MESH,
+        )
+
+    moves = [mate_copy(i) for i in range(4)]
+    moves.append(
+        pltpu.make_async_remote_copy(
+            lists_ref,
+            mate_lists,
+            mate_send.at[4],
+            mate_recv.at[4],
+            device_id=mate,
+            device_id_type=MESH,
+        )
+    )
+    for i in (4, 0, 1, 2, 3):
+        moves[i].start()
+    for copy in metas:
+        copy.wait_recv()
+
+    def flags(target):
+        return [
+            meta_ref[0:1, :] == target,
+            meta_ref[1:2, :] == target,
+            metas_ref[0, 0:1, :] == target,
+            metas_ref[0, 1:2, :] == target,
+        ]
+
+    def chosen_points(target, part):
+        total = None
+        for flag, (ref, slot) in zip(
+            flags(target), [(points_ref, 0), (points_ref, 1), (mate_points, 0), (mate_points, 1)]
+        ):
+            keep = jnp.where(flag, 1.0, 0.0).astype(jnp.bfloat16)
+            term = ref[pl.ds(slot * rows + part * half, half), :] * keep
+            total = term if total is None else total + term
+        return total
+
+    def chosen_lists(target):
+        total = None
+        for flag, (ref, slot) in zip(
+            flags(target), [(lists_ref, 0), (lists_ref, 1), (mate_lists, 0), (mate_lists, 1)]
+        ):
+            keep = jnp.where(flag, 1, 0)
+            keep = jnp.concatenate([keep] * (rows // keep.shape[1]), axis=1)
+            term = ref[:, slot * rows : (slot + 1) * rows] * keep
+            total = term if total is None else total + term
+        return total
+
+    target = over[0]
+    sends = [
+        pltpu.make_async_remote_copy(
+            source,
+            landing,
+            over_send.at[i],
+            over_recv.at[i],
+            device_id=over,
+            device_id_type=MESH,
+        )
+        for i, (source, landing) in enumerate(
+            [
+                (out_points.at[pl.ds(0, half)], in_points.at[pl.ds(0, half)]),
+                (out_points.at[pl.ds(half, half)], in_points.at[pl.ds(half, half)]),
+                (out_lists, in_lists),
+            ]
+        )
+    ]
+    moves[4].wait_recv()
+    out_lists[...] = chosen_lists(target)
+    sends[2].start()
+    for part in range(2):
+        moves[2 * part].wait_recv()
+        moves[2 * part + 1].wait_recv()
+        out_points[pl.ds(part * half, half), :] = chosen_points(target, part)
+        sends[part].start()
+    metas_out[...] = metas_ref[...]
+    ours = chosen_lists(me)
+    for part in range(2):
+        points_out[pl.ds(part * half, half), :] = chosen_points(me, part)
+    sends[2].wait_recv()
+    lists_out[...] = (ours + in_lists[...]) * (points_ref.shape[1] // 128)
+    for part in range(2):
+        sends[part].wait_recv()
+        span = pl.ds(part * half, half)
+        points_out[span, :] = points_out[span, :] + in_points[span, :]
+    for copy in metas + moves + sends:
+        copy.wait_send()
+
+
+def to_owners(points, lists, meta, owners):
+    rows, width = points.shape[0] // 2, points.shape[1]
+    fanout = lists.shape[0]
+    vmem = pl.BlockSpec(memory_space=pltpu.VMEM)
+    count = owners + 2
+    return pl.pallas_call(
+        functools.partial(owners_kernel, owners),
+        out_shape=(
+            jax.ShapeDtypeStruct((rows, width), points.dtype),
+            jax.ShapeDtypeStruct((fanout, rows), jnp.int32),
+            jax.ShapeDtypeStruct((count + 1,) + meta.shape, jnp.int32),
+        ),
+        in_specs=[vmem] * 3,
+        out_specs=(vmem,) * 3,
+        scratch_shapes=[
+            pltpu.VMEM(points.shape, points.dtype),
+            pltpu.VMEM(lists.shape, jnp.int32),
+            pltpu.VMEM((rows, width), points.dtype),
+            pltpu.VMEM((fanout, rows), jnp.int32),
+            pltpu.VMEM((rows, width), points.dtype),
+            pltpu.VMEM((fanout, rows), jnp.int32),
+            pltpu.VMEM((count + 1,) + meta.shape, jnp.int32),
+            pltpu.SemaphoreType.DMA((count,)),
+            pltpu.SemaphoreType.DMA((count,)),
+            pltpu.SemaphoreType.DMA((5,)),
+            pltpu.SemaphoreType.DMA((5,)),
+            pltpu.SemaphoreType.DMA((3,)),
+            pltpu.SemaphoreType.DMA((3,)),
+        ],
+        compiler_params=pltpu.CompilerParams(
+            collective_id=0, has_side_effects=True, vmem_limit_bytes=56 * 1024 * 1024
+        ),
+        cost_estimate=pl.CostEstimate(flops=1 << 20, bytes_accessed=8 << 20, transcendentals=0),
+        name="to_owners",
+    )(points, lists, meta)
+
+
+def encode_kernel(
     fetch_ref,
     order_ref,
     near_ref,
@@ -27,11 +233,8 @@
     lists_ref,
     depth_ref,
     turned_ref,
-    mixing_ref,
-    gain_ref,
-    qkv_ref,
-    out_w_ref,
-    out_ref,
+    features_ref,
+    encoded_ref,
     x_ref,
     xt_ref,
     fine_ref,
@@ -40,17 +243,10 @@
     wide_ref,
     acc_ref,
     code_ref,
-    updated_ref,
-    qt_ref,
-    k_ref,
-    vt_ref,
-    mixed_ref,
-    result_ref,
 ):
     rows, width = x_ref.shape
     fanout = depth_ref.shape[0]
     in_blocks = fetch_ref.shape[0]
-    out_blocks = order_ref.shape[0]
     piece = rows // in_blocks
     chunks = rows // CHUNK
     lanes = 128
@@ -104,12 +300,48 @@
                 + sums_ref[pl.ds(i, CHUNK, stride=parts), :]
             ).astype(jnp.bfloat16)
 
+    for b in range(in_blocks):
+        here = pl.ds(pl.multiple_of(order_ref[b] * piece, piece), piece)
+        features_ref[pl.ds(b * piece, piece), :] = x_ref[here, :]
+        encoded_ref[pl.ds(b * piece, piece), :] = code_ref[here, :]
+
+
+def attention_kernel(
+    mode,
+    owners,
+    x_ref,
+    code_ref,
+    mixing_ref,
+    gain_ref,
+    qkv_ref,
+    out_w_ref,
+    out_ref,
+    updated_ref,
+    qt_ref,
+    k_ref,
+    vt_ref,
+    mixed_ref,
+    result_ref,
+    *extra,
+):
+    rows, width = x_ref.shape
+    lanes = 128
+    chunks = rows // CHUNK
+    if mode != "alone":
+        me, mine = lax.axis_index("grp"), lax.axis_index("dev")
+        landed_ref, turn_send, turn_recv = extra[:3]
+        peers = [(me, around(owners, mine, k)) for k in range(1, owners)]
+        if mode == "home":
+            mate, over, _ = neighbours_of(4, owners)
+            peers += [mate, over]
+        entered = greet(peers)
     gain = gain_ref[...]
     scale = HEAD_DIM**-0.5 * math.log2(math.e)
 
     @pl.loop(0, chunks)
     def _(c):
         here = pl.ds(pl.multiple_of(c * CHUNK, CHUNK), CHUNK)
+
         updated = x_ref[here, :].astype(jnp.float32) + jnp.dot(
             code_ref[here, :], mixing_ref[...], preferred_element_type=jnp.float32
         )
@@ -126,6 +358,33 @@
             vt_ref[h, :HEAD_DIM, here] = values[h * HEAD_DIM : (h + 1) * HEAD_DIM]
 
     vt_ref[:, HEAD_DIM:, :] = jnp.ones((HEADS, ONES, rows), jnp.bfloat16)
+
+    if mode != "alone":
+        share = rows // owners
+
+        def outgoing(k):
+            return pltpu.make_async_remote_copy(
+                result_ref.at[pl.ds(pl.multiple_of(k * share, share), share)],
+                landed_ref.at[pl.ds(pl.multiple_of(mine * share, share), share)],
+                turn_send.at[k],
+                turn_recv.at[k],
+                device_id=(me, around(owners, mine, k + 1)),
+                device_id_type=MESH,
+            )
+
+        def arriving(k):
+            return pltpu.make_async_remote_copy(
+                result_ref.at[pl.ds(pl.multiple_of(k * share, share), share)],
+                landed_ref.at[
+                    pl.ds(pl.multiple_of(around(owners, mine, -1 - k) * share, share), share)
+                ],
+                turn_send.at[k],
+                turn_recv.at[k],
+                device_id=(me, around(owners, mine, k + 1)),
+                device_id_type=MESH,
+            )
+
+        entered()
 
     @pl.loop(0, chunks)
     def _(c):
@@ -157,26 +416,99 @@
             updated_ref[here, :]
             + jnp.dot(mixed, out_w_ref[...], preferred_element_type=jnp.float32)
         ).astype(jnp.bfloat16)
-
-    for b in range(out_blocks):
-        out_ref[pl.ds(b * piece, piece), :] = result_ref[
-            pl.ds(pl.multiple_of(order_ref[b] * piece, piece), piece), :
-        ]
-
-
-def run_block(source, lines, params, fetch, order, rows):
+        if mode != "alone":
+            for i in range(CHUNK // share):
+                k = c * (CHUNK // share) + i
+
+                @pl.when(k < owners - 1)
+                def _():
+                    outgoing(k).start()
+
+    if mode == "alone":
+        out_ref[...] = result_ref[...]
+        return
+    landed_ref[pl.ds(pl.multiple_of(mine * share, share), share), :] = result_ref[
+        pl.ds((owners - 1) * share, share), :
+    ]
+    if mode == "regroup":
+        for k in range(owners - 1):
+            arriving(k).wait_recv()
+        out_ref[...] = landed_ref[...]
+        for k in range(owners - 1):
+            outgoing(k).wait_send()
+        return
+
+    over_send, over_recv, own_send, own_recv, far_send, far_recv = extra[3:]
+
+    def onward(i, source, landing, send, recv, device):
+        sender = mine if i == 0 else around(owners, mine, -i)
+        at = pl.multiple_of(sender * share, share)
+        return pltpu.make_async_remote_copy(
+            landed_ref.at[pl.ds(source * rows + at, share)],
+            landed_ref.at[pl.ds(landing * rows + at, share)],
+            send.at[i],
+            recv.at[i],
+            device_id=device,
+            device_id_type=MESH,
+        )
+
+    overs = [onward(i, 0, 1, over_send, over_recv, over) for i in range(owners)]
+    owns = [onward(i, 0, 2, own_send, own_recv, mate) for i in range(owners)]
+    fars = [onward(i, 1, 3, far_send, far_recv, mate) for i in range(owners)]
+    for i in range(owners + 1):
+        if i < owners:
+            if i > 0:
+                arriving(i - 1).wait_recv()
+            overs[i].start()
+            owns[i].start()
+        if i > 0:
+            overs[i - 1].wait_recv()
+            fars[i - 1].start()
+    for copy in owns + fars:
+        copy.wait_recv()
+    out_ref[...] = landed_ref[...]
+    for copy in overs + owns + fars:
+        copy.wait_send()
+    for k in range(owners - 1):
+        outgoing(k).wait_send()
+
+
+def place_kernel(home_ref, source_ref, out_ref):
+    pieces = home_ref.shape[0]
+    piece = out_ref.shape[0] // pieces
+    last = source_ref.shape[0] // piece
+    for b in range(pieces):
+        live = home_ref[b] < last
+        here = pl.multiple_of(jnp.minimum(home_ref[b], last - 1) * piece, piece)
+        found = source_ref[pl.ds(here, piece), :]
+        out_ref[pl.ds(b * piece, piece), :] = jnp.where(live, found, jnp.zeros_like(found))
+
+
+def put_home(source, home, piece):
+    vmem = pl.BlockSpec(memory_space=pltpu.VMEM)
+    return pl.pallas_call(
+        place_kernel,
+        out_shape=jax.ShapeDtypeStruct((home.shape[0] * piece, source.shape[1]), source.dtype),
+        in_specs=[pl.BlockSpec(memory_space=pltpu.SMEM), vmem],
+        out_specs=vmem,
+        compiler_params=pltpu.CompilerParams(vmem_limit_bytes=LIMIT),
+        name="put_home",
+    )(home, source)
+
+
+def run_block(source, lines, params, fetch, order, rows, mode="alone", owners=1):
     depth, mixing, gain, w_qkv, w_out = params
     width = source.shape[1]
     fanout = lines.shape[0]
-    piece = rows // fetch.shape[0]
     parts = width // 128
     vmem = pl.BlockSpec(memory_space=pltpu.VMEM)
     smem = pl.BlockSpec(memory_space=pltpu.SMEM)
-    return pl.pallas_call(
-        block_kernel,
-        out_shape=jax.ShapeDtypeStruct((order.shape[0] * piece, width), jnp.bfloat16),
-        in_specs=[smem] * 3 + [vmem] * 8,
-        out_specs=vmem,
+    patch = jax.ShapeDtypeStruct((rows, width), jnp.bfloat16)
+    features, encoded = pl.pallas_call(
+        encode_kernel,
+        out_shape=(patch, patch),
+        in_specs=[smem] * 3 + [vmem] * 4,
+        out_specs=(vmem, vmem),
         scratch_shapes=[
             pltpu.VMEM((rows, width), jnp.bfloat16),
             pltpu.VMEM((width, rows), jnp.bfloat16),
@@ -186,31 +518,49 @@
             pltpu.VMEM((PRODUCTS, width, 128), jnp.float32),
             pltpu.VMEM((width, CHUNK), jnp.float32),
             pltpu.VMEM((rows, width), jnp.bfloat16),
+        ],
+        compiler_params=pltpu.CompilerParams(vmem_limit_bytes=LIMIT),
+        cost_estimate=pl.CostEstimate(
+            flops=2 * fanout * rows * rows * width, bytes_accessed=4 << 20, transcendentals=0
+        ),
+        name="encode",
+    )(fetch, order, lines, source, lines, depth, depth.T)
+    extra = []
+    settings = pltpu.CompilerParams(vmem_limit_bytes=LIMIT)
+    copies = 4 if mode == "home" else 1
+    if mode != "alone":
+        extra = [
+            pltpu.VMEM((copies * rows, width), jnp.bfloat16),
+            pltpu.SemaphoreType.DMA((owners - 1,)),
+            pltpu.SemaphoreType.DMA((owners - 1,)),
+        ]
+        settings = pltpu.CompilerParams(
+            vmem_limit_bytes=LIMIT,
+            collective_id=1 if mode == "regroup" else 2,
+            has_side_effects=True,
+        )
+    if mode == "home":
+        extra += [pltpu.SemaphoreType.DMA((owners,))] * 6
+    return pl.pallas_call(
+        functools.partial(attention_kernel, mode, owners),
+        out_shape=jax.ShapeDtypeStruct((copies * rows, width), jnp.bfloat16),
+        in_specs=[vmem] * 6,
+        out_specs=vmem,
+        scratch_shapes=[
             pltpu.VMEM((rows, width), jnp.float32),
             pltpu.VMEM((width, rows), jnp.bfloat16),
             pltpu.VMEM((rows, width), jnp.bfloat16),
             pltpu.VMEM((HEADS, HEAD_DIM + ONES, rows), jnp.bfloat16),
             pltpu.VMEM((width, CHUNK), jnp.float32),
             pltpu.VMEM((rows, width), jnp.bfloat16),
-        ],
-        compiler_params=pltpu.CompilerParams(vmem_limit_bytes=56 * 1024 * 1024),
+        ]
+        + extra,
+        compiler_params=settings,
         cost_estimate=pl.CostEstimate(
-            flops=2 * fanout * rows * rows * width, bytes_accessed=8 << 20, transcendentals=8 << 20
+            flops=10 * rows * width * width, bytes_accessed=8 << 20, transcendentals=8 << 20
         ),
-        name="block",
-    )(
-        fetch,
-        order,
-        lines,
-        source,
-        lines,
-        depth,
-        depth.T,
-        mixing,
-        gain.reshape(1, width),
-        w_qkv,
-        w_out,
-    )
+        name="attention_" + mode,
+    )(features, encoded, mixing, gain.reshape(1, width), w_qkv, w_out)
 
 
 def body(
@@ -247,6 +597,64 @@
     first_params = (depth_first, mixing_first, gain_first, w_qkv_first, w_out_first)
     second_params = (depth_second, mixing_second, gain_second, w_qkv_second, w_out_second)
 
+    if chips == 2 and slot_count == 2 and owners * CAPACITY == block_count:
+        filled = jnp.arange(slot_count) < counts[0]
+        wanted = jnp.where(filled, owner_group, -1)
+        meta = jnp.concatenate(
+            [
+                jnp.broadcast_to(wanted[:, None], (slot_count, width)),
+                jnp.broadcast_to(
+                    jnp.pad(hilbert_target, (0, width - block_count))[None], (6, width)
+                ),
+            ]
+        ).astype(jnp.int32)
+        points, lines, metas = to_owners(home_points, neighbors_home, meta, owners)
+        counter = jnp.arange(block_count)
+
+        def slot_places(table):
+            aim = table // block_count
+            same = aim[:, :, None] == aim[:, None, :]
+            rank = jnp.sum(same & (counter[:, None] > counter[None, :]), axis=2)
+            return aim, rank
+
+        told = metas[:, slot_count, :block_count]
+        aim, rank = slot_places(told)
+        turn = ((aim[3] - mine - 1) % owners) * CAPACITY + rank[3]
+        order = jnp.sum(
+            jnp.where(turn[None, :] == counter[:, None], counter[None, :], 0), axis=1
+        ).astype(jnp.int32)
+        straight = jnp.arange(block_count, dtype=jnp.int32)
+        incoming = run_block(
+            points, lines, first_params, straight, order, rows, "regroup", owners
+        )
+        sender = (mine - jnp.arange(owners)) % owners
+        sent_at = (sender[:, None] * CAPACITY + rank[3:]).reshape(-1)
+        goal = mine * block_count + counter
+        fetch = jnp.sum(
+            jnp.where(told[3:].reshape(-1)[None, :] == goal[:, None], sent_at[None, :], 0), axis=1
+        ).astype(jnp.int32)
+        wheel = (counter + (mine + 1) * CAPACITY) % block_count
+        back = jnp.sum(
+            jnp.where(fetch[None, :] == wheel[:, None], counter[None, :], 0), axis=1
+        ).astype(jnp.int32)
+        places = aim * CAPACITY + rank
+        places = jnp.stack([places[3], places[1], places[0], places[2]])
+        buffer = (owner_group // CORES != place_x) + 2 * (owner_group % CORES != core)
+        home = jnp.where(
+            filled[:, None], buffer[:, None] * block_count + places[buffer], 4 * block_count
+        )
+        buffers = run_block(
+            incoming,
+            neighbors_second * (width // 128),
+            second_params,
+            fetch,
+            back,
+            rows,
+            "home",
+            owners,
+        )
+        return put_home(buffers, home.reshape(-1).astype(jnp.int32), piece)
+
     targets = lax.all_gather(hilbert_target, "dev", axis=0, tiled=True).reshape(
         owners, block_count
     )
@@ -310,10 +718,16 @@
     ).astype(jnp.int32)
 
     straight = jnp.arange(block_count, dtype=jnp.int32)
-    outgoing = run_block(points, stamps[:fanout] * (width // 128), first_params, straight, order, rows)
+    section_one = run_block(
+        points, stamps[:fanout] * (width // 128), first_params, straight, straight, rows
+    )
+    outgoing = section_one.reshape(block_count, piece, width)[order].reshape(-1, width)
     swap = lambda a: lax.all_to_all(a, "dev", split_axis=0, concat_axis=0, tiled=True)
     incoming = swap(outgoing)
-    backward = run_block(incoming, neighbors_second * (width // 128), second_params, fetch, back, rows)
+    section_two = run_block(
+        incoming, neighbors_second * (width // 128), second_params, fetch, straight, rows
+    )
+    backward = section_two.reshape(block_count, piece, width)[back].reshape(-1, width)
     returned = swap(backward).reshape(slots, piece, width)
     finished = returned[place].reshape(rows, width)
 

time: 265 us -> 219 us (0.83)
  Pallas kernels: 113 us -> 205 us
  waiting for transfers between devices: 75.6 us -> 0 us
  starting transfers between devices: 18.4 us -> 0 us
  other arithmetic: 24.1 us -> 5.84 us
  between operations: 13.3 us -> 0.76 us
  local copies, waits for them, and re-layouts: 12.5 us -> 6.75 us
  blocking collectives: 5.42 us -> 0 us
    pallas_call x2 -> x6, Pallas kernels: 113 us -> 205 us  [the longest x2 90.3 us: run_block(): pl.pallas_call(functools.partial(attention_kernel, mode, owners), out_sha...]
    all_to_all x2 -> x0, waiting for transfers between devices: 42 us -> none  [body(): lax.all_to_all(a, 'dev', split_axis=0, concat_axis=0, tiled=True)]
    ppermute x6 -> x0, waiting for transfers between devices: 33.6 us -> none  [the longest x1 21.7 us: body(): gathered.append(lax.ppermute(finished, 'grp', over))]
    select_n x7 -> x4, other arithmetic: 13.9 us -> 0.1 us  [the longest x1 0.07 us: body(): jnp.where(filled[:, None], buffer[:, None] * block_count + places[buffer]...]
    all_to_all x2 -> x0, starting transfers between devices: 12.2 us -> none  [body(): lax.all_to_all(a, 'dev', split_axis=0, concat_axis=0, tiled=True)]
    ppermute x6 -> x0, starting transfers between devices: 6.23 us -> none  [the longest x1 2.66 us: body(): other = lax.ppermute(stack, 'grp', mate)]
    unnamed x1 -> x0, blocking collectives: 5.42 us -> none
    unnamed x25 -> x5, local copies, waits for them, and re-layouts: 6.98 us -> 3.39 us
  transfers between devices with their start and end apart: 8 -> 0, of which waited for: 4 -> 0; matrix products, arithmetic and copies ran while one was open for 8% -> 0% of each run, Pallas kernels for 0% -> 0%
where the time goes in v2:
time: 219 us; the launch traced here: 218 us
  Pallas kernels  205 us (94%)
  local copies, waits for them, and re-layouts  6.75 us (3%)
  other arithmetic  5.84 us (3%)
    pallas_call x2, Pallas kernels, run_block(): pl.pallas_call(functools.partial(attention_kernel, mode, owners), out_sha...  90.3 us
    pallas_call x2, Pallas kernels, run_block(): pl.pallas_call(encode_kernel, out_shape=(patch, patch), in_specs=[smem] *...  75.8 us
    pallas_call x1, Pallas kernels, to_owners(): pl.pallas_call(functools.partial(owners_kernel, owners), out_shape=(jax.S...  35.2 us

profile of v2, /device:TPU:25, one launch (start us, length us, event | category | flops | bytes accessed | tf_op | source)
XLA Modules:
  0.0 218.3 jit_solution(6901591615361390479)
XLA Ops:
  0.7 0.6 iota.41.fetch_ref
  1.3 0.7 broadcast_multiply_fusion.1
  2.0 0.7 pad.4
  2.7 0.7 pad_add_fusion.meta_ref
  3.3 1.6 broadcast_multiply_fusion.near_ref.lists_ref
  4.9 1.7 copy.19
  6.6 1.7 copy.20
  8.3 35.2 %to_owners.1 = (bf16[1024,512]{1,0:T(8,128)(2,1)}, s32[27,1024]{1,0:T(8,128)}, s32[11,8,512]{2,1,0:T(8,128)}) custom-call(bf16[2048,512]{1,0:T(8,128)(2,1)} %points_ref.1, s32[27,2048]{1,0:T(8,128)} %lists_ref.1, s32[8,512]{1,0:T(8,128)} %pad_add_fusion.meta_ref), custom_call_target="tpu_custom_call" | custom-call | flops 1048576 | bytes 8388608 | tf_op jit(solution)/shard_map/to_owners/pallas_call | solution.py:196
  43.4 0.8 slice_reduce_fusion
  44.2 0.8 fusion.13
  45.0 0.1 eq.69
  45.1 0.4 convert_reduce_fusion
  45.5 0.7 select_reduce_fusion.order_ref
  46.2 0.1 slice_add_fusion
  46.3 0.1 broadcast_in_dim.77
  46.3 0.2 select_reduce_fusion.2.fetch_ref
  46.5 0.0 copy-start
  46.5 0.7 select_reduce_fusion.1.order_ref
  47.2 0.6 gather_fusion
  47.8 0.1 add_select_fusion.1
  47.9 0.6 select_n.94.home_ref
  48.5 38.0 %encode.2 = (bf16[1024,512]{1,0:T(8,128)(2,1)}, bf16[1024,512]{1,0:T(8,128)(2,1)}) custom-call(s32[16]{0:T(128)} %iota.41.fetch_ref, s32[16]{0:T(128)} %select_reduce_fusion.order_ref, s32[27,1024]{1,0:T(8,128)} %get-tuple-element.13.near_ref.lists_ref, bf16[1024,512]{1,0:T(8,128)(2,1)} %get-tuple-element.14.source_ref, ...), custom_call_target="tpu_custom_call" | custom-call | flops 28991029248 | bytes 4194304 | tf_op jit(solution)/shard_map/encode/pallas_call | solution.py:507
  86.5 0.0 copy-done
  86.5 33.3 %attention_regroup.1.source_ref = bf16[1024,512]{1,0:T(8,128)(2,1)} custom-call(bf16[1024,512]{1,0:T(8,128)(2,1)} %get-tuple-element.15.x_ref, bf16[1024,512]{1,0:T(8,128)(2,1)} %get-tuple-element.16.code_ref, bf16[512,512]{1,0:T(8,128)(2,1)} %mixing_ref.2, f32[1,512]{1,0:T(1,128)} %bitcast.33, bf16[512,1536]{1,0:T(8,128)(2,1)} %qkv_ref.2, ...), custom_call_target="tpu_custom_call" | custom-call | flops 2684354560 | bytes 8388608 | tf_op jit(solution)/shard_map/attention_regroup/pallas_call | solution.py:544
  119.8 37.8 %encode.3 = (bf16[1024,512]{1,0:T(8,128)(2,1)}, bf16[1024,512]{1,0:T(8,128)(2,1)}) custom-call(s32[16]{0:T(128)} %copy-done, s32[16]{0:T(128)} %select_reduce_fusion.1.order_ref, s32[27,1024]{1,0:T(8,128)} %broadcast_multiply_fusion.near_ref.lists_ref, bf16[1024,512]{1,0:T(8,128)(2,1)} %attention_regroup.1.source_ref, ...), custom_call_target="tpu_custom_call" | custom-call | flops 28991029248 | bytes 4194304 | tf_op jit(solution)/shard_map/encode/pallas_call | solution.py:507
  157.5 57.1 %attention_home.1.source_ref = bf16[4096,512]{1,0:T(8,128)(2,1)} custom-call(bf16[1024,512]{1,0:T(8,128)(2,1)} %get-tuple-element.17.x_ref, bf16[1024,512]{1,0:T(8,128)(2,1)} %get-tuple-element.18.code_ref, bf16[512,512]{1,0:T(8,128)(2,1)} %mixing_ref.3, f32[1,512]{1,0:T(1,128)} %bitcast.34, bf16[512,1536]{1,0:T(8,128)(2,1)} %qkv_ref.3, ...), custom_call_target="tpu_custom_call" | custom-call | flops 2684354560 | bytes 8388608 | tf_op jit(solution)/shard_map/attention_home/pallas_call | solution.py:544
  214.6 3.7 %put_home.1 = bf16[2048,512]{1,0:T(8,128)(2,1)} custom-call(s32[32]{0:T(128)} %select_n.94.home_ref, bf16[4096,512]{1,0:T(8,128)(2,1)} %attention_home.1.source_ref), custom_call_target="tpu_custom_call" | custom-call | tf_op jit(solution)/shard_map/put_home/pallas_call | solution.py:489
  (15 shorter events, 0.1 us)
Async XLA Ops:
  46.5 40.0 %copy-start = (s32[16]{0:T(128)}, s32[16]{0:T(128)S(1)}, u32[]{:S(2)}) copy-start(s32[16]{0:T(128)S(1)} %select_reduce_fusion.2.fetch_ref) | copy-start | bytes 196

commit v3 on v2

--- a/solution.py
+++ b/solution.py
@@ -15,8 +15,8 @@
 CHUNK = 256
 EPSILON = 1e-05
 ONES = 16
-PRODUCTS = 12
-STEP = 3
+TURNS = 4
+QUARTERS = 4
 LIMIT = 56 * 1024 * 1024
 
 
@@ -51,6 +51,8 @@
     points_out,
     lists_out,
     metas_out,
+    give_points,
+    give_lists,
     mate_points,
     mate_lists,
     out_points,
@@ -67,125 +69,107 @@
 ):
     me, mine = lax.axis_index("grp"), lax.axis_index("dev")
     rows = points_out.shape[0]
-    half = rows // 2
+    part = rows // QUARTERS
     mate, over, slant = neighbours_of(4, owners)
-    column = [mate, over, slant]
-    line = [(me, around(owners, mine, k)) for k in range(1, owners)]
-    peers = column + line
+    peers = [mate, over, slant] + [(me, around(owners, mine, k)) for k in range(1, owners)]
     entered = greet(peers)
+
+    def flags(target):
+        return [meta_ref[slot : slot + 1, :] == target for slot in range(2)]
+
+    def chosen_points(target, q):
+        one, two = [jnp.where(f, 1.0, 0.0).astype(jnp.bfloat16) for f in flags(target)]
+        return (
+            points_ref[pl.ds(q * part, part), :] * one
+            + points_ref[pl.ds(rows + q * part, part), :] * two
+        )
+
+    def chosen_lists(target):
+        one, two = [
+            jnp.concatenate([jnp.where(f, 1, 0)] * (rows // f.shape[1]), axis=1)
+            for f in flags(target)
+        ]
+        return lists_ref[:, :rows] * one + lists_ref[:, rows:] * two
+
+    def copy(source, landing, send, recv, i, device):
+        return pltpu.make_async_remote_copy(
+            source, landing, send.at[i], recv.at[i], device_id=device, device_id_type=MESH
+        )
+
+    metas = [
+        copy(meta_ref, metas_ref.at[i if i < 3 else i + 1], meta_send, meta_recv, i, peer)
+        for i, peer in enumerate(peers)
+    ]
+    spans = [pl.ds(q * part, part) for q in range(QUARTERS)]
+    gives = [
+        [
+            copy(
+                give_points.at[half, span],
+                mate_points.at[half, span],
+                mate_send,
+                mate_recv,
+                half * QUARTERS + q,
+                mate,
+            )
+            for q, span in enumerate(spans)
+        ]
+        + [
+            copy(
+                give_lists.at[half],
+                mate_lists.at[half],
+                mate_send,
+                mate_recv,
+                2 * QUARTERS + half,
+                mate,
+            )
+        ]
+        for half in range(2)
+    ]
+    sends = [
+        copy(out_points.at[span], in_points.at[span], over_send, over_recv, q, over)
+        for q, span in enumerate(spans)
+    ] + [copy(out_lists, in_lists, over_send, over_recv, QUARTERS, over)]
+
     entered()
-
-    def meta_copy(i, slot):
-        return pltpu.make_async_remote_copy(
-            meta_ref,
-            metas_ref.at[slot],
-            meta_send.at[i],
-            meta_recv.at[i],
-            device_id=peers[i],
-            device_id_type=MESH,
-        )
-
-    count = len(peers)
-    metas = [meta_copy(i, i if i < 3 else i + 1) for i in range(count)]
-    for copy in metas:
-        copy.start()
+    for q, span in enumerate(spans):
+        give_points[0, span] = chosen_points(slant[0], q)
+        gives[0][q].start()
+    give_lists[0] = chosen_lists(slant[0])
+    gives[0][QUARTERS].start()
+    for move in metas:
+        move.start()
     metas_ref[3] = meta_ref[...]
-
-    def mate_copy(i):
-        slot, part = i % 2, i // 2
-        span = pl.ds(slot * rows + part * half, half)
-        return pltpu.make_async_remote_copy(
-            points_ref.at[span],
-            mate_points.at[span],
-            mate_send.at[i],
-            mate_recv.at[i],
-            device_id=mate,
-            device_id_type=MESH,
-        )
-
-    moves = [mate_copy(i) for i in range(4)]
-    moves.append(
-        pltpu.make_async_remote_copy(
-            lists_ref,
-            mate_lists,
-            mate_send.at[4],
-            mate_recv.at[4],
-            device_id=mate,
-            device_id_type=MESH,
-        )
-    )
-    for i in (4, 0, 1, 2, 3):
-        moves[i].start()
-    for copy in metas:
-        copy.wait_recv()
-
-    def flags(target):
-        return [
-            meta_ref[0:1, :] == target,
-            meta_ref[1:2, :] == target,
-            metas_ref[0, 0:1, :] == target,
-            metas_ref[0, 1:2, :] == target,
-        ]
-
-    def chosen_points(target, part):
-        total = None
-        for flag, (ref, slot) in zip(
-            flags(target), [(points_ref, 0), (points_ref, 1), (mate_points, 0), (mate_points, 1)]
-        ):
-            keep = jnp.where(flag, 1.0, 0.0).astype(jnp.bfloat16)
-            term = ref[pl.ds(slot * rows + part * half, half), :] * keep
-            total = term if total is None else total + term
-        return total
-
-    def chosen_lists(target):
-        total = None
-        for flag, (ref, slot) in zip(
-            flags(target), [(lists_ref, 0), (lists_ref, 1), (mate_lists, 0), (mate_lists, 1)]
-        ):
-            keep = jnp.where(flag, 1, 0)
-            keep = jnp.concatenate([keep] * (rows // keep.shape[1]), axis=1)
-            term = ref[:, slot * rows : (slot + 1) * rows] * keep
-            total = term if total is None else total + term
-        return total
-
-    target = over[0]
-    sends = [
-        pltpu.make_async_remote_copy(
-            source,
-            landing,
-            over_send.at[i],
-            over_recv.at[i],
-            device_id=over,
-            device_id_type=MESH,
-        )
-        for i, (source, landing) in enumerate(
-            [
-                (out_points.at[pl.ds(0, half)], in_points.at[pl.ds(0, half)]),
-                (out_points.at[pl.ds(half, half)], in_points.at[pl.ds(half, half)]),
-                (out_lists, in_lists),
-            ]
-        )
-    ]
-    moves[4].wait_recv()
-    out_lists[...] = chosen_lists(target)
-    sends[2].start()
-    for part in range(2):
-        moves[2 * part].wait_recv()
-        moves[2 * part + 1].wait_recv()
-        out_points[pl.ds(part * half, half), :] = chosen_points(target, part)
-        sends[part].start()
+    for q, span in enumerate(spans):
+        kept = chosen_points(over[0], q)
+        gives[0][q].wait_recv()
+        out_points[span, :] = kept + mate_points[0, span]
+        sends[q].start()
+    kept = chosen_lists(over[0])
+    gives[0][QUARTERS].wait_recv()
+    out_lists[...] = kept + mate_lists[0]
+    sends[QUARTERS].start()
+    for q, span in enumerate(spans):
+        give_points[1, span] = chosen_points(mate[0], q)
+        gives[1][q].start()
+    give_lists[1] = chosen_lists(mate[0])
+    gives[1][QUARTERS].start()
+    for q, span in enumerate(spans):
+        kept = chosen_points(me, q)
+        gives[1][q].wait_recv()
+        points_out[span, :] = kept + mate_points[1, span]
+    kept = chosen_lists(me)
+    gives[1][QUARTERS].wait_recv()
+    kept = kept + mate_lists[1]
+    for move in metas:
+        move.wait_recv()
     metas_out[...] = metas_ref[...]
-    ours = chosen_lists(me)
-    for part in range(2):
-        points_out[pl.ds(part * half, half), :] = chosen_points(me, part)
-    sends[2].wait_recv()
-    lists_out[...] = (ours + in_lists[...]) * (points_ref.shape[1] // 128)
-    for part in range(2):
-        sends[part].wait_recv()
-        span = pl.ds(part * half, half)
+    for q, span in enumerate(spans):
+        sends[q].wait_recv()
         points_out[span, :] = points_out[span, :] + in_points[span, :]
-    for copy in metas + moves + sends:
-        copy.wait_send()
+    sends[QUARTERS].wait_recv()
+    lists_out[...] = (kept + in_lists[...]) * (points_ref.shape[1] // 128)
+    for move in metas + gives[0] + gives[1] + sends:
+        move.wait_send()
 
 
 def to_owners(points, lists, meta, owners):
@@ -203,8 +187,10 @@
         in_specs=[vmem] * 3,
         out_specs=(vmem,) * 3,
         scratch_shapes=[
-            pltpu.VMEM(points.shape, points.dtype),
-            pltpu.VMEM(lists.shape, jnp.int32),
+            pltpu.VMEM((2, rows, width), points.dtype),
+            pltpu.VMEM((2, fanout, rows), jnp.int32),
+            pltpu.VMEM((2, rows, width), points.dtype),
+            pltpu.VMEM((2, fanout, rows), jnp.int32),
             pltpu.VMEM((rows, width), points.dtype),
             pltpu.VMEM((fanout, rows), jnp.int32),
             pltpu.VMEM((rows, width), points.dtype),
@@ -212,10 +198,10 @@
             pltpu.VMEM((count + 1,) + meta.shape, jnp.int32),
             pltpu.SemaphoreType.DMA((count,)),
             pltpu.SemaphoreType.DMA((count,)),
-            pltpu.SemaphoreType.DMA((5,)),
-            pltpu.SemaphoreType.DMA((5,)),
-            pltpu.SemaphoreType.DMA((3,)),
-            pltpu.SemaphoreType.DMA((3,)),
+            pltpu.SemaphoreType.DMA((2 * QUARTERS + 2,)),
+            pltpu.SemaphoreType.DMA((2 * QUARTERS + 2,)),
+            pltpu.SemaphoreType.DMA((QUARTERS + 1,)),
+            pltpu.SemaphoreType.DMA((QUARTERS + 1,)),
         ],
         compiler_params=pltpu.CompilerParams(
             collective_id=0, has_side_effects=True, vmem_limit_bytes=56 * 1024 * 1024
@@ -226,6 +212,7 @@
 
 
 def encode_kernel(
+    products,
     fetch_ref,
     order_ref,
     near_ref,
@@ -261,23 +248,23 @@
             jnp.float32
         )
         slim_ref[pl.ds(c, fanout, stride=parts), :] = depth_ref[:, c * lanes : (c + 1) * lanes]
-    for j in range(PRODUCTS):
+    for j in range(products):
         wide_ref[j] = jnp.broadcast_to(turned_ref[:, j : j + 1], (width, lanes))
     places = (lax.broadcasted_iota(jnp.int32, (rows, CHUNK), 0) * parts).astype(jnp.int16)
     one, nil = jnp.bfloat16(1), jnp.bfloat16(0)
-    turns = PRODUCTS // STEP
-    points = CHUNK // turns
+    step = products // TURNS
+    points = CHUNK // TURNS
 
     @pl.loop(0, chunks)
     def _(c):
         at = pl.multiple_of(c * CHUNK, CHUNK)
         acc_ref[...] = jnp.zeros_like(acc_ref)
 
-        @pl.loop(0, turns)
+        @pl.loop(0, TURNS)
         def _(t):
             total = acc_ref[...]
-            for dj in range(STEP):
-                j = t * STEP + dj
+            for dj in range(step):
+                j = t * step + dj
                 row = lists_ref[pl.ds(j, 1), pl.ds(at, CHUNK)].astype(jnp.int16)
                 hot = jnp.where(places == row, one, nil)
                 got = jnp.dot(xt_ref[...], hot, preferred_element_type=jnp.float32)
@@ -285,12 +272,13 @@
                 total = total + got * jnp.concatenate([weight] * (CHUNK // lanes), axis=1)
             acc_ref[...] = total
             first = t * points
-            weights = [slim_ref[pl.ds(j * parts, parts), :] for j in range(PRODUCTS, fanout)]
+            base = (c * TURNS + t) * (fanout * points)
+            weights = [slim_ref[pl.ds(j * parts, parts), :] for j in range(products, fanout)]
             for p in range(points):
                 total = None
-                for j in range(PRODUCTS, fanout):
-                    line = pl.multiple_of(near_ref[j, at + first + p], parts)
-                    term = fine_ref[pl.ds(line, parts), :] * weights[j - PRODUCTS]
+                for j in range(products, fanout):
+                    line = pl.multiple_of(near_ref[base + (j * points + p)], parts)
+                    term = fine_ref[pl.ds(line, parts), :] * weights[j - products]
                     total = term if total is None else total + term
                 sums_ref[pl.ds(pl.multiple_of((first + p) * parts, parts), parts), :] = total
 
@@ -368,7 +356,7 @@
                 landed_ref.at[pl.ds(pl.multiple_of(mine * share, share), share)],
                 turn_send.at[k],
                 turn_recv.at[k],
-                device_id=(me, around(owners, mine, k + 1)),
+                device_id=(me, around(owners, mine, k)),
                 device_id_type=MESH,
             )
 
@@ -376,14 +364,43 @@
             return pltpu.make_async_remote_copy(
                 result_ref.at[pl.ds(pl.multiple_of(k * share, share), share)],
                 landed_ref.at[
-                    pl.ds(pl.multiple_of(around(owners, mine, -1 - k) * share, share), share)
+                    pl.ds(pl.multiple_of(around(owners, mine, -k) * share, share), share)
                 ],
                 turn_send.at[k],
                 turn_recv.at[k],
-                device_id=(me, around(owners, mine, k + 1)),
+                device_id=(me, around(owners, mine, k)),
                 device_id_type=MESH,
             )
 
+        if mode == "home":
+            over_send, over_recv, own_send, own_recv, far_send, far_recv = extra[3:]
+
+        def onward(k, source, landing, send, recv, device):
+            at = pl.multiple_of(around(owners, mine, -k) * share, share)
+            return pltpu.make_async_remote_copy(
+                landed_ref.at[pl.ds(source * rows + at, share)],
+                landed_ref.at[pl.ds(landing * rows + at, share)],
+                send.at[k],
+                recv.at[k],
+                device_id=device,
+                device_id_type=MESH,
+            )
+
+        def to_over(k):
+            return onward(k, 0, 1, over_send, over_recv, over)
+
+        def to_mate(k):
+            return onward(k, 0, 2, own_send, own_recv, mate)
+
+        def far_to_mate(k):
+            return onward(k, 1, 3, far_send, far_recv, mate)
+
+        def forward(k):
+            arriving(k).wait_recv()
+            to_over(k).start()
+            to_mate(k).start()
+
+        each = CHUNK // share
         entered()
 
     @pl.loop(0, chunks)
@@ -416,60 +433,67 @@
             updated_ref[here, :]
             + jnp.dot(mixed, out_w_ref[...], preferred_element_type=jnp.float32)
         ).astype(jnp.bfloat16)
-        if mode != "alone":
-            for i in range(CHUNK // share):
-                k = c * (CHUNK // share) + i
-
-                @pl.when(k < owners - 1)
-                def _():
-                    outgoing(k).start()
+        if mode == "alone":
+            return
+
+        @pl.when(c == 0)
+        def _():
+            landed_ref[pl.ds(pl.multiple_of(mine * share, share), share), :] = result_ref[
+                pl.ds(0, share), :
+            ]
+            for k in range(1, each):
+                outgoing(k).start()
+            if mode == "home":
+                to_over(0).start()
+                to_mate(0).start()
+
+        @pl.when(c > 0)
+        def _():
+            for i in range(each):
+                outgoing(c * each + i).start()
+
+        if mode == "home":
+
+            @pl.when(c == 1)
+            def _():
+                for k in range(1, each):
+                    forward(k)
+
+            @pl.when(c > 1)
+            def _():
+                for i in range(each):
+                    forward((c - 1) * each + i)
 
     if mode == "alone":
         out_ref[...] = result_ref[...]
         return
-    landed_ref[pl.ds(pl.multiple_of(mine * share, share), share), :] = result_ref[
-        pl.ds((owners - 1) * share, share), :
-    ]
     if mode == "regroup":
-        for k in range(owners - 1):
+        for k in range(1, owners):
             arriving(k).wait_recv()
         out_ref[...] = landed_ref[...]
-        for k in range(owners - 1):
+        for k in range(1, owners):
             outgoing(k).wait_send()
         return
 
-    over_send, over_recv, own_send, own_recv, far_send, far_recv = extra[3:]
-
-    def onward(i, source, landing, send, recv, device):
-        sender = mine if i == 0 else around(owners, mine, -i)
-        at = pl.multiple_of(sender * share, share)
-        return pltpu.make_async_remote_copy(
-            landed_ref.at[pl.ds(source * rows + at, share)],
-            landed_ref.at[pl.ds(landing * rows + at, share)],
-            send.at[i],
-            recv.at[i],
-            device_id=device,
-            device_id_type=MESH,
-        )
-
-    overs = [onward(i, 0, 1, over_send, over_recv, over) for i in range(owners)]
-    owns = [onward(i, 0, 2, own_send, own_recv, mate) for i in range(owners)]
-    fars = [onward(i, 1, 3, far_send, far_recv, mate) for i in range(owners)]
-    for i in range(owners + 1):
-        if i < owners:
-            if i > 0:
-                arriving(i - 1).wait_recv()
-            overs[i].start()
-            owns[i].start()
-        if i > 0:
-            overs[i - 1].wait_recv()
-            fars[i - 1].start()
-    for copy in owns + fars:
-        copy.wait_recv()
+    done = 0
+    for k in range(owners - each, owners):
+        while done < k - 2:
+            to_over(done).wait_recv()
+            far_to_mate(done).start()
+            done += 1
+        forward(k)
+    for k in range(done, owners):
+        to_over(k).wait_recv()
+        far_to_mate(k).start()
+    for k in range(owners):
+        to_mate(k).wait_recv()
+        far_to_mate(k).wait_recv()
     out_ref[...] = landed_ref[...]
-    for copy in overs + owns + fars:
-        copy.wait_send()
-    for k in range(owners - 1):
+    for k in range(owners):
+        to_over(k).wait_send()
+        to_mate(k).wait_send()
+        far_to_mate(k).wait_send()
+    for k in range(1, owners):
         outgoing(k).wait_send()
 
 
@@ -496,7 +520,7 @@
     )(home, source)
 
 
-def run_block(source, lines, params, fetch, order, rows, mode="alone", owners=1):
+def run_block(source, lines, params, fetch, order, rows, products, mode="alone", owners=1):
     depth, mixing, gain, w_qkv, w_out = params
     width = source.shape[1]
     fanout = lines.shape[0]
@@ -504,8 +528,9 @@
     vmem = pl.BlockSpec(memory_space=pltpu.VMEM)
     smem = pl.BlockSpec(memory_space=pltpu.SMEM)
     patch = jax.ShapeDtypeStruct((rows, width), jnp.bfloat16)
+    near = lines.reshape(fanout, -1, CHUNK // TURNS).transpose(1, 0, 2).reshape(-1)
     features, encoded = pl.pallas_call(
-        encode_kernel,
+        functools.partial(encode_kernel, products),
         out_shape=(patch, patch),
         in_specs=[smem] * 3 + [vmem] * 4,
         out_specs=(vmem, vmem),
@@ -515,7 +540,7 @@
             pltpu.VMEM((rows * parts, 128), jnp.float32),
             pltpu.VMEM((fanout * parts, 128), jnp.float32),
             pltpu.VMEM((CHUNK * parts, 128), jnp.float32),
-            pltpu.VMEM((PRODUCTS, width, 128), jnp.float32),
+            pltpu.VMEM((products, width, 128), jnp.float32),
             pltpu.VMEM((width, CHUNK), jnp.float32),
             pltpu.VMEM((rows, width), jnp.bfloat16),
         ],
@@ -524,15 +549,15 @@
             flops=2 * fanout * rows * rows * width, bytes_accessed=4 << 20, transcendentals=0
         ),
         name="encode",
-    )(fetch, order, lines, source, lines, depth, depth.T)
+    )(fetch, order, near, source, lines, depth, depth.T)
     extra = []
     settings = pltpu.CompilerParams(vmem_limit_bytes=LIMIT)
     copies = 4 if mode == "home" else 1
     if mode != "alone":
         extra = [
             pltpu.VMEM((copies * rows, width), jnp.bfloat16),
-            pltpu.SemaphoreType.DMA((owners - 1,)),
-            pltpu.SemaphoreType.DMA((owners - 1,)),
+            pltpu.SemaphoreType.DMA((owners,)),
+            pltpu.SemaphoreType.DMA((owners,)),
         ]
         settings = pltpu.CompilerParams(
             vmem_limit_bytes=LIMIT,
@@ -619,13 +644,14 @@
 
         told = metas[:, slot_count, :block_count]
         aim, rank = slot_places(told)
-        turn = ((aim[3] - mine - 1) % owners) * CAPACITY + rank[3]
+        own_aim, own_rank = slot_places(hilbert_target[None])
+        turn = ((own_aim[0] - mine) % owners) * CAPACITY + own_rank[0]
         order = jnp.sum(
             jnp.where(turn[None, :] == counter[:, None], counter[None, :], 0), axis=1
         ).astype(jnp.int32)
         straight = jnp.arange(block_count, dtype=jnp.int32)
         incoming = run_block(
-            points, lines, first_params, straight, order, rows, "regroup", owners
+            points, lines, first_params, straight, order, rows, 16, "regroup", owners
         )
         sender = (mine - jnp.arange(owners)) % owners
         sent_at = (sender[:, None] * CAPACITY + rank[3:]).reshape(-1)
@@ -633,7 +659,7 @@
         fetch = jnp.sum(
             jnp.where(told[3:].reshape(-1)[None, :] == goal[:, None], sent_at[None, :], 0), axis=1
         ).astype(jnp.int32)
-        wheel = (counter + (mine + 1) * CAPACITY) % block_count
+        wheel = (counter + mine * CAPACITY) % block_count
         back = jnp.sum(
             jnp.where(fetch[None, :] == wheel[:, None], counter[None, :], 0), axis=1
         ).astype(jnp.int32)
@@ -650,6 +676,7 @@
             fetch,
             back,
             rows,
+            20,
             "home",
             owners,
         )
@@ -719,13 +746,13 @@
 
     straight = jnp.arange(block_count, dtype=jnp.int32)
     section_one = run_block(
-        points, stamps[:fanout] * (width // 128), first_params, straight, straight, rows
+        points, stamps[:fanout] * (width // 128), first_params, straight, straight, rows, 16
     )
     outgoing = section_one.reshape(block_count, piece, width)[order].reshape(-1, width)
     swap = lambda a: lax.all_to_all(a, "dev", split_axis=0, concat_axis=0, tiled=True)
     incoming = swap(outgoing)
     section_two = run_block(
-        incoming, neighbors_second * (width // 128), second_params, fetch, straight, rows
+        incoming, neighbors_second * (width // 128), second_params, fetch, straight, rows, 16
     )
     backward = section_two.reshape(block_count, piece, width)[back].reshape(-1, width)
     returned = swap(backward).reshape(slots, piece, width)

time: 219 us -> 222 us (1.014)
  local copies, waits for them, and re-layouts: 6.75 us -> 9.38 us
    pallas_call x2, Pallas kernels: 90.3 us -> 94.4 us  [run_block(): pl.pallas_call(functools.partial(attention_kernel, mode, owners), out_sha...]
    pallas_call x2, Pallas kernels: 75.8 us -> 72.2 us  [run_block(): pl.pallas_call(functools.partial(encode_kernel, products), out_shape=(pat...]
    reshape x0 -> x6, local copies, waits for them, and re-layouts: none -> 2.73 us  [run_block(): lines.reshape(fanout, -1, CHUNK // TURNS).transpose(1, 0, 2).reshape(-1)]
where the time goes in v3:
time: 222 us; the launch traced here: 221 us
  Pallas kernels  204 us (92%)
  local copies, waits for them, and re-layouts  9.38 us (4%)
  other arithmetic  6.78 us (3%)
    pallas_call x2, Pallas kernels, run_block(): pl.pallas_call(functools.partial(attention_kernel, mode, owners), out_sha...  94.4 us
    pallas_call x2, Pallas kernels, run_block(): pl.pallas_call(functools.partial(encode_kernel, products), out_shape=(pat...  72.2 us
    pallas_call x1, Pallas kernels, to_owners(): pl.pallas_call(functools.partial(owners_kernel, owners), out_shape=(jax.S...  33.8 us

profile of v3, /device:TPU:25, one launch (start us, length us, event | category | flops | bytes accessed | tf_op | source)
XLA Modules:
  0.0 221.0 jit_solution(5533059390464753014)
XLA Ops:
  0.7 0.7 and_select_fusion.2
  1.3 0.2 convert_reduce_fusion.1
  1.5 0.7 fusion.7
  2.2 0.6 select_reduce_fusion.order_ref
  2.9 0.5 iota.48.fetch_ref
  3.3 0.7 broadcast_multiply_fusion.1
  4.0 0.7 pad.4
  4.7 0.7 pad_add_fusion.meta_ref
  5.4 0.9 broadcast_multiply_fusion.lists_ref
  6.3 0.0 copy-start
  6.3 0.1 reshape.219
  6.4 0.1 copy.50
  6.5 0.7 reshape.220.near_ref
  7.2 1.7 copy.25
  8.9 1.7 copy.26
  10.6 33.8 %to_owners.1 = (bf16[1024,512]{1,0:T(8,128)(2,1)}, s32[27,1024]{1,0:T(8,128)}, s32[11,8,512]{2,1,0:T(8,128)}) custom-call(bf16[2048,512]{1,0:T(8,128)(2,1)} %points_ref.1, s32[27,2048]{1,0:T(8,128)} %lists_ref.1, s32[8,512]{1,0:T(8,128)} %pad_add_fusion.meta_ref), custom_call_target="tpu_custom_call" | custom-call | flops 1048576 | bytes 8388608 | tf_op jit(solution)/shard_map/to_owners/pallas_call | solution.py:180
  44.4 0.0 copy-done
  44.4 0.8 slice_reduce_fusion
  45.2 0.8 fusion.12
  46.0 0.1 eq.88
  46.1 0.4 convert_reduce_fusion
  46.5 0.1 slice_add_fusion
  46.6 0.1 broadcast_in_dim.49
  46.7 0.2 select_reduce_fusion.2.fetch_ref
  46.8 0.0 copy-start.1
  46.8 0.8 select_reduce_fusion.1.order_ref
  47.6 0.6 gather_fusion
  48.2 0.1 add_select_fusion.1
  48.3 0.6 select_n.101.home_ref
  48.9 1.0 reshape.221
  49.9 0.1 copy.49
  50.0 0.7 reshape.222.near_ref
  50.7 35.4 %encode.2 = (bf16[1024,512]{1,0:T(8,128)(2,1)}, bf16[1024,512]{1,0:T(8,128)(2,1)}) custom-call(s32[16]{0:T(128)} %iota.48.fetch_ref, s32[16]{0:T(128)} %select_reduce_fusion.order_ref, s32[27648]{0:T(1024)} %reshape.222.near_ref, bf16[1024,512]{1,0:T(8,128)(2,1)} %get-tuple-element.14.source_ref, s32[27,1024]{1,0:T(8,128)} %get-tuple-element.13.lists_ref, ...), custom_call_target="tpu_custom_call" | custom-call | flops 28991029248 | bytes 4194304 | tf_op jit(solution)/shard_map/encode/pallas_call | solution.py:532
  86.1 0.0 copy-done.1
  86.1 37.7 %attention_regroup.1.source_ref = bf16[1024,512]{1,0:T(8,128)(2,1)} custom-call(bf16[1024,512]{1,0:T(8,128)(2,1)} %get-tuple-element.15.x_ref, bf16[1024,512]{1,0:T(8,128)(2,1)} %get-tuple-element.16.code_ref, bf16[512,512]{1,0:T(8,128)(2,1)} %mixing_ref.2, f32[1,512]{1,0:T(1,128)} %bitcast.39, bf16[512,1536]{1,0:T(8,128)(2,1)} %qkv_ref.2, ...), custom_call_target="tpu_custom_call" | custom-call | flops 2684354560 | bytes 8388608 | tf_op jit(solution)/shard_map/attention_regroup/pallas_call | solution.py:569
  123.8 36.7 %encode.3 = (bf16[1024,512]{1,0:T(8,128)(2,1)}, bf16[1024,512]{1,0:T(8,128)(2,1)}) custom-call(s32[16]{0:T(128)} %copy-done.1, s32[16]{0:T(128)} %select_reduce_fusion.1.order_ref, s32[27648]{0:T(1024)} %reshape.220.near_ref, bf16[1024,512]{1,0:T(8,128)(2,1)} %attention_regroup.1.source_ref, s32[27,1024]{1,0:T(8,128)} %copy-done, f32[27,512]{1,0:T(8,128)} %depth_ref.3, ...), custom_call_target="tpu_custom_call" | custom-call | flops 28991029248 | bytes 4194304 | tf_op jit(solution)/shard_map/encode/pallas_call | solution.py:532
  160.6 56.7 %attention_home.1.source_ref = bf16[4096,512]{1,0:T(8,128)(2,1)} custom-call(bf16[1024,512]{1,0:T(8,128)(2,1)} %get-tuple-element.17.x_ref, bf16[1024,512]{1,0:T(8,128)(2,1)} %get-tuple-element.18.code_ref, bf16[512,512]{1,0:T(8,128)(2,1)} %mixing_ref.3, f32[1,512]{1,0:T(1,128)} %bitcast.40, bf16[512,1536]{1,0:T(8,128)(2,1)} %qkv_ref.3, ...), custom_call_target="tpu_custom_call" | custom-call | flops 2684354560 | bytes 8388608 | tf_op jit(solution)/shard_map/attention_home/pallas_call | solution.py:569
  217.3 3.7 %put_home.1 = bf16[2048,512]{1,0:T(8,128)(2,1)} custom-call(s32[32]{0:T(128)} %select_n.101.home_ref, bf16[4096,512]{1,0:T(8,128)(2,1)} %attention_home.1.source_ref), custom_call_target="tpu_custom_call" | custom-call | tf_op jit(solution)/shard_map/put_home/pallas_call | solution.py:513
  (14 shorter events, 0.1 us)
Async XLA Ops:
  6.3 38.1 %copy-start = (s32[27,1024]{1,0:T(8,128)}, s32[27,1024]{1,0:T(8,128)S(1)}, u32[]{:S(2)}) copy-start(s32[27,1024]{1,0:T(8,128)S(1)} %broadcast_multiply_fusion.lists_ref) | copy-start | bytes 331780
  46.8 39.3 %copy-start.1 = (s32[16]{0:T(128)}, s32[16]{0:T(128)S(1)}, u32[]{:S(2)}) copy-start(s32[16]{0:T(128)S(1)} %select_reduce_fusion.2.fetch_ref) | copy-start | bytes 196

commit v4 on v3

--- a/solution.py
+++ b/solution.py
@@ -213,13 +213,13 @@
 
 def encode_kernel(
     products,
+    cuts,
     fetch_ref,
     order_ref,
     near_ref,
     source_ref,
     lists_ref,
     depth_ref,
-    turned_ref,
     features_ref,
     encoded_ref,
     x_ref,
@@ -230,6 +230,7 @@
     wide_ref,
     acc_ref,
     code_ref,
+    tall_ref,
 ):
     rows, width = x_ref.shape
     fanout = depth_ref.shape[0]
@@ -248,8 +249,11 @@
             jnp.float32
         )
         slim_ref[pl.ds(c, fanout, stride=parts), :] = depth_ref[:, c * lanes : (c + 1) * lanes]
+    tall_ref[...] = jnp.zeros_like(tall_ref)
+    tall_ref[:fanout, :] = depth_ref[...]
+    turned = tall_ref[...].T
     for j in range(products):
-        wide_ref[j] = jnp.broadcast_to(turned_ref[:, j : j + 1], (width, lanes))
+        wide_ref[j] = jnp.broadcast_to(turned[:, j : j + 1], (width, lanes))
     places = (lax.broadcasted_iota(jnp.int32, (rows, CHUNK), 0) * parts).astype(jnp.int16)
     one, nil = jnp.bfloat16(1), jnp.bfloat16(0)
     step = products // TURNS
@@ -262,25 +266,26 @@
 
         @pl.loop(0, TURNS)
         def _(t):
-            total = acc_ref[...]
-            for dj in range(step):
-                j = t * step + dj
-                row = lists_ref[pl.ds(j, 1), pl.ds(at, CHUNK)].astype(jnp.int16)
-                hot = jnp.where(places == row, one, nil)
-                got = jnp.dot(xt_ref[...], hot, preferred_element_type=jnp.float32)
-                weight = wide_ref[j]
-                total = total + got * jnp.concatenate([weight] * (CHUNK // lanes), axis=1)
-            acc_ref[...] = total
             first = t * points
             base = (c * TURNS + t) * (fanout * points)
             weights = [slim_ref[pl.ds(j * parts, parts), :] for j in range(products, fanout)]
-            for p in range(points):
-                total = None
-                for j in range(products, fanout):
-                    line = pl.multiple_of(near_ref[base + (j * points + p)], parts)
-                    term = fine_ref[pl.ds(line, parts), :] * weights[j - products]
-                    total = term if total is None else total + term
-                sums_ref[pl.ds(pl.multiple_of((first + p) * parts, parts), parts), :] = total
+            pieces = step * cuts
+            deep = rows // cuts
+            for i in range(pieces):
+                j = t * step + i // cuts
+                span = slice(i % cuts * deep, (i % cuts + 1) * deep)
+                row = lists_ref[pl.ds(j, 1), pl.ds(at, CHUNK)].astype(jnp.int16)
+                hot = jnp.where(places[span] == row, one, nil)
+                got = jnp.dot(xt_ref[:, span], hot, preferred_element_type=jnp.float32)
+                weight = wide_ref[j]
+                acc_ref[...] += got * jnp.concatenate([weight] * (CHUNK // lanes), axis=1)
+                for p in range(i * points // pieces, (i + 1) * points // pieces):
+                    total = None
+                    for near in range(products, fanout):
+                        line = pl.multiple_of(near_ref[base + (near * points + p)], parts)
+                        term = fine_ref[pl.ds(line, parts), :] * weights[near - products]
+                        total = term if total is None else total + term
+                    sums_ref[pl.ds(pl.multiple_of((first + p) * parts, parts), parts), :] = total
 
         for i in range(parts):
             code_ref[pl.ds(at, CHUNK), i * lanes : (i + 1) * lanes] = (
@@ -520,7 +525,7 @@
     )(home, source)
 
 
-def run_block(source, lines, params, fetch, order, rows, products, mode="alone", owners=1):
+def run_block(source, lines, params, fetch, order, rows, products, cuts, mode="alone", owners=1):
     depth, mixing, gain, w_qkv, w_out = params
     width = source.shape[1]
     fanout = lines.shape[0]
@@ -530,9 +535,9 @@
     patch = jax.ShapeDtypeStruct((rows, width), jnp.bfloat16)
     near = lines.reshape(fanout, -1, CHUNK // TURNS).transpose(1, 0, 2).reshape(-1)
     features, encoded = pl.pallas_call(
-        functools.partial(encode_kernel, products),
+        functools.partial(encode_kernel, products, cuts),
         out_shape=(patch, patch),
-        in_specs=[smem] * 3 + [vmem] * 4,
+        in_specs=[smem] * 3 + [vmem] * 3,
         out_specs=(vmem, vmem),
         scratch_shapes=[
             pltpu.VMEM((rows, width), jnp.bfloat16),
@@ -543,13 +548,14 @@
             pltpu.VMEM((products, width, 128), jnp.float32),
             pltpu.VMEM((width, CHUNK), jnp.float32),
             pltpu.VMEM((rows, width), jnp.bfloat16),
+            pltpu.VMEM((128, width), jnp.float32),
         ],
         compiler_params=pltpu.CompilerParams(vmem_limit_bytes=LIMIT),
         cost_estimate=pl.CostEstimate(
             flops=2 * fanout * rows * rows * width, bytes_accessed=4 << 20, transcendentals=0
         ),
         name="encode",
-    )(fetch, order, near, source, lines, depth, depth.T)
+    )(fetch, order, near, source, lines, depth)
     extra = []
     settings = pltpu.CompilerParams(vmem_limit_bytes=LIMIT)
     copies = 4 if mode == "home" else 1
@@ -651,7 +657,7 @@
         ).astype(jnp.int32)
         straight = jnp.arange(block_count, dtype=jnp.int32)
         incoming = run_block(
-            points, lines, first_params, straight, order, rows, 16, "regroup", owners
+            points, lines, first_params, straight, order, rows, 12, 4, "regroup", owners
         )
         sender = (mine - jnp.arange(owners)) % owners
         sent_at = (sender[:, None] * CAPACITY + rank[3:]).reshape(-1)
@@ -676,7 +682,8 @@
             fetch,
             back,
             rows,
-            20,
+            12,
+            2,
             "home",
             owners,
         )
@@ -746,13 +753,13 @@
 
     straight = jnp.arange(block_count, dtype=jnp.int32)
     section_one = run_block(
-        points, stamps[:fanout] * (width // 128), first_params, straight, straight, rows, 16
+        points, stamps[:fanout] * (width // 128), first_params, straight, straight, rows, 12, 4
     )
     outgoing = section_one.reshape(block_count, piece, width)[order].reshape(-1, width)
     swap = lambda a: lax.all_to_all(a, "dev", split_axis=0, concat_axis=0, tiled=True)
     incoming = swap(outgoing)
     section_two = run_block(
-        incoming, neighbors_second * (width // 128), second_params, fetch, straight, rows, 16
+        incoming, neighbors_second * (width // 128), second_params, fetch, straight, rows, 12, 4
     )
     backward = section_two.reshape(block_count, piece, width)[back].reshape(-1, width)
     returned = swap(backward).reshape(slots, piece, width)

time: 222 us -> 205 us (0.923)
  Pallas kernels: 204 us -> 191 us
  local copies, waits for them, and re-layouts: 9.38 us -> 6.03 us
    pallas_call x2, Pallas kernels: 72.2 us -> 58.9 us  [run_block(): pl.pallas_call(functools.partial(encode_kernel, products, cuts), out_shap...]
    unnamed x7 -> x5, local copies, waits for them, and re-layouts: 3.39 us -> 0.01 us
where the time goes in v4:
time: 205 us; the launch traced here: 204 us
  Pallas kernels  191 us (93%)
  other arithmetic  6.83 us (3%)
  local copies, waits for them, and re-layouts  6.03 us (3%)
    pallas_call x2, Pallas kernels, run_block(): pl.pallas_call(functools.partial(attention_kernel, mode, owners), out_sha...  94.4 us
    pallas_call x2, Pallas kernels, run_block(): pl.pallas_call(functools.partial(encode_kernel, products, cuts), out_shap...  58.9 us
    pallas_call x1, Pallas kernels, to_owners(): pl.pallas_call(functools.partial(owners_kernel, owners), out_shape=(jax.S...  33.7 us

profile of v4, /device:TPU:25, one launch (start us, length us, event | category | flops | bytes accessed | tf_op | source)
XLA Modules:
  0.0 204.3 jit_solution(17479509558791907416)
XLA Ops:
  0.7 0.7 and_select_fusion.2
  1.3 0.2 convert_reduce_fusion.1
  1.5 0.7 fusion.7
  2.2 0.7 select_reduce_fusion.order_ref
  2.9 0.5 iota.48.fetch_ref
  3.4 0.7 broadcast_multiply_fusion.1
  4.1 0.7 pad.4
  4.8 0.7 pad_add_fusion.meta_ref
  5.5 0.9 broadcast_multiply_fusion.lists_ref
  6.4 0.0 copy-start
  6.4 0.1 reshape.219
  6.5 0.1 copy.44
  6.6 0.7 reshape.220.near_ref
  7.3 33.7 %to_owners.1 = (bf16[1024,512]{1,0:T(8,128)(2,1)}, s32[27,1024]{1,0:T(8,128)}, s32[11,8,512]{2,1,0:T(8,128)}) custom-call(bf16[2048,512]{1,0:T(8,128)(2,1)} %points_ref.1, s32[27,2048]{1,0:T(8,128)} %lists_ref.1, s32[8,512]{1,0:T(8,128)} %pad_add_fusion.meta_ref), custom_call_target="tpu_custom_call" | custom-call | flops 1048576 | bytes 8388608 | tf_op jit(solution)/shard_map/to_owners/pallas_call | solution.py:180
  41.1 0.8 slice_reduce_fusion
  41.9 0.8 fusion.12
  42.7 0.1 eq.88
  42.8 0.4 convert_reduce_fusion
  43.2 0.1 slice_add_fusion
  43.2 0.1 broadcast_in_dim.49
  43.3 0.2 select_reduce_fusion.2.fetch_ref
  43.5 0.0 copy-start.1
  43.5 0.8 select_reduce_fusion.1.order_ref
  44.3 0.6 gather_fusion
  44.9 0.1 add_select_fusion.1
  44.9 0.6 select_n.101.home_ref
  45.5 1.0 reshape.221
  46.6 0.1 copy.43
  46.6 0.0 copy-done
  46.6 0.7 reshape.222.near_ref
  47.4 30.7 %encode.2 = (bf16[1024,512]{1,0:T(8,128)(2,1)}, bf16[1024,512]{1,0:T(8,128)(2,1)}) custom-call(s32[16]{0:T(128)} %iota.48.fetch_ref, s32[16]{0:T(128)} %select_reduce_fusion.order_ref, s32[27648]{0:T(1024)} %reshape.222.near_ref, bf16[1024,512]{1,0:T(8,128)(2,1)} %get-tuple-element.14.source_ref, s32[27,1024]{1,0:T(8,128)} %get-tuple-element.13.lists_ref, ...), custom_call_target="tpu_custom_call" | custom-call | flops 28991029248 | bytes 4194304 | tf_op jit(solution)/shard_map/encode/pallas_call | solution.py:537
  78.0 0.0 copy-done.1
  78.0 37.6 %attention_regroup.1.source_ref = bf16[1024,512]{1,0:T(8,128)(2,1)} custom-call(bf16[1024,512]{1,0:T(8,128)(2,1)} %get-tuple-element.15.x_ref, bf16[1024,512]{1,0:T(8,128)(2,1)} %get-tuple-element.16.code_ref, bf16[512,512]{1,0:T(8,128)(2,1)} %mixing_ref.2, f32[1,512]{1,0:T(1,128)} %bitcast.35, bf16[512,1536]{1,0:T(8,128)(2,1)} %qkv_ref.2, ...), custom_call_target="tpu_custom_call" | custom-call | flops 2684354560 | bytes 8388608 | tf_op jit(solution)/shard_map/attention_regroup/pallas_call | solution.py:575
  115.7 28.2 %encode.3 = (bf16[1024,512]{1,0:T(8,128)(2,1)}, bf16[1024,512]{1,0:T(8,128)(2,1)}) custom-call(s32[16]{0:T(128)} %copy-done.1, s32[16]{0:T(128)} %select_reduce_fusion.1.order_ref, s32[27648]{0:T(1024)} %reshape.220.near_ref, bf16[1024,512]{1,0:T(8,128)(2,1)} %attention_regroup.1.source_ref, s32[27,1024]{1,0:T(8,128)} %copy-done, f32[27,512]{1,0:T(8,128)} %depth_ref.3), custom_call_target="tpu_custom_call" | custom-call | flops 28991029248 | bytes 4194304 | tf_op jit(solution)/shard_map/encode/pallas_call | solution.py:537
  143.9 56.8 %attention_home.1.source_ref = bf16[4096,512]{1,0:T(8,128)(2,1)} custom-call(bf16[1024,512]{1,0:T(8,128)(2,1)} %get-tuple-element.17.x_ref, bf16[1024,512]{1,0:T(8,128)(2,1)} %get-tuple-element.18.code_ref, bf16[512,512]{1,0:T(8,128)(2,1)} %mixing_ref.3, f32[1,512]{1,0:T(1,128)} %bitcast.36, bf16[512,1536]{1,0:T(8,128)(2,1)} %qkv_ref.3, ...), custom_call_target="tpu_custom_call" | custom-call | flops 2684354560 | bytes 8388608 | tf_op jit(solution)/shard_map/attention_home/pallas_call | solution.py:575
  200.7 3.7 %put_home.1 = bf16[2048,512]{1,0:T(8,128)(2,1)} custom-call(s32[32]{0:T(128)} %select_n.101.home_ref, bf16[4096,512]{1,0:T(8,128)(2,1)} %attention_home.1.source_ref), custom_call_target="tpu_custom_call" | custom-call | tf_op jit(solution)/shard_map/put_home/pallas_call | solution.py:518
  (14 shorter events, 0.1 us)
Async XLA Ops:
  6.4 40.2 %copy-start = (s32[27,1024]{1,0:T(8,128)}, s32[27,1024]{1,0:T(8,128)S(1)}, u32[]{:S(2)}) copy-start(s32[27,1024]{1,0:T(8,128)S(1)} %broadcast_multiply_fusion.lists_ref) | copy-start | bytes 331780
  43.5 34.5 %copy-start.1 = (s32[16]{0:T(128)}, s32[16]{0:T(128)S(1)}, u32[]{:S(2)}) copy-start(s32[16]{0:T(128)S(1)} %select_reduce_fusion.2.fetch_ref) | copy-start | bytes 196
